TPU v7x, 128 devices: a whole 4x4x4 slice. The times are simulated.
128 devices in a mesh: gx: 4 (over x_lo, core), gy: 4 (over y), gz: 8 (over x_hi, z).
Axes of the slice: x: 4 (x_hi: 2, x_lo: 2; x = x_hi * 2 + x_lo), y: 4, z: 4, core: 2. Of those that a mesh axis runs over, the one named last changes fastest.
Arguments:
- positions: float32 [3, 2048, 128], P(None, ('gx', 'gy', 'gz')), may hold values from -6 to 6
- velocities: float32 [3, 2048, 128], P(None, ('gx', 'gy', 'gz')), may hold values from -6 to 6
- weights: float32 [2048, 128], P(('gx', 'gy', 'gz')), may hold values from 0.5 to 2
- counts: int32 [2048], P(('gx', 'gy', 'gz')), may hold values from 32 to 128
- link_offset: int32 [2048, 3], P(('gx', 'gy', 'gz')), may hold values from -16 to 16
- link_mask: int32 [2048, 3], P(('gx', 'gy', 'gz')), may hold values 0 or 1
- bin_box: int32 [2048, 1], P(('gx', 'gy', 'gz')), may hold values from 0 to 15; in each aligned block of 16 rows (0 to 15, 16 to 31, ...) at most 2 rows name the same one
- bin_cell: int32 [2048], P(('gx', 'gy', 'gz')), may hold values from 0 to 4095
- fluid: float32 [3, 16, 32, 1024], P(None, 'gx', 'gy', 'gz'), may hold values from -6 to 6
Outputs:
- positions_out: float32 [3, 2048, 128], P(None, ('gx', 'gy', 'gz'))
- velocities_out: float32 [3, 2048, 128], P(None, ('gx', 'gy', 'gz'))
- fluid_out: float32 [3, 16, 32, 1024], P(None, 'gx', 'gy', 'gz')
Inputs may be any that keep to these rules, and one draw needn't show every extreme that they name: `bin_box`: the bins of one device name one value at most 2 times; the cell lies in the box at the bin owner's index of gz. `bin_cell`: index of the cell inside its box, first dimension slowest. Slots 0 to counts - 1 of a bin are occupied.
All inputs are finite; a program needn't handle non-finite values. No bound on the sum of `link_mask` on one device may be relied on, other than what follows from the above.
Results may differ from a plain program's by a relative error of at most 0.0001.
Values sent between devices are 32-bit elements; how exact they have to be, the bound alone decides.
A program may use at most 128 MiB of HBM per device.

v0:
```python
import jax
import jax.numpy as jnp
from jax import lax
from jax.sharding import PartitionSpec as P

SUBSTEPS = 2


step_sub = 0.1
stiffness = 0.05
damping = 0.05
drag_rate = 1.0
coupling = 0.004
viscosity = 0.12
highest = lax.Precision.HIGHEST


def padded_2(cells, sides, width):
    for axis, dim in sides:
        count = lax.axis_size(axis)
        ends = count - 1
        head = lax.slice_in_dim(cells, 0, width, axis=dim)
        tail = lax.slice_in_dim(cells, cells.shape[dim] - width, cells.shape[dim], axis=dim)
        cells = jnp.concatenate(
            [
                lax.ppermute(tail, axis, [(i, (i + 1) % count) for i in range(ends)]),
                cells,
                lax.ppermute(head, axis, [((i + 1) % count, i) for i in range(ends)]),
            ],
            axis=dim,
        )
    return cells


def contact(own_pos, own_vel, near_pos, near_vel, near_weight):
    distance = jnp.zeros(
        near_weight.shape[:2] + (own_pos.shape[2], near_weight.shape[2]), jnp.float32
    )
    for component in range(3):
        offset = own_pos[component][:, None, :, None] - near_pos[component][:, :, None, :]
        distance = distance + offset * offset
    kernel = near_weight[:, :, None, :] * jnp.exp(-0.5 * distance)
    weight_sum = jnp.sum(kernel, axis=(1, 3))
    pull_pos = jnp.einsum("bqij,cbqj->cbi", kernel, near_pos, precision=highest)
    pull_vel = jnp.einsum("bqij,cbqj->cbi", kernel, near_vel, precision=highest)
    return stiffness * (own_pos * weight_sum[None] - pull_pos) - damping * (
        own_vel * weight_sum[None] - pull_vel
    )


def advance(
    widened, state_pos, state_vel, carried, occupied, fluid_seen, neighbour, link_weight, block_bins
):
    bin_count = state_pos.shape[1]

    def one_block(block_id, running):
        nearby = widened[:, neighbour]
        near_pos = jnp.concatenate([state_pos[:, :, None], nearby[0:3]], 2)
        near_vel = jnp.concatenate([state_vel[:, :, None], nearby[3:6]], 2)
        near_weight = jnp.concatenate([carried[:, None], nearby[6] * link_weight[:, :, None]], 1)
        contact_force = contact(state_pos, state_vel, near_pos, near_vel, near_weight)
        drag_force = drag_rate * (fluid_seen[:, :, None] - state_vel)
        moved_vel = state_vel + step_sub * occupied[None] * (contact_force + drag_force)
        moved_pos = state_pos + step_sub * occupied[None] * moved_vel
        pulled_block = jnp.sum(carried[None] * drag_force, axis=2)
        return (moved_pos, moved_vel, pulled_block)

    start_state = (
        jnp.zeros_like(state_pos),
        jnp.zeros_like(state_vel),
        jnp.zeros((3, bin_count), jnp.float32),
    )
    return lax.fori_loop(0, bin_count // block_bins, one_block, start_state)


def stencil(padded):
    centre = padded[:, 1:-1, 1:-1, 1:-1]
    beside_all = padded[:, 2:, 1:-1, 1:-1] + padded[:, :-2, 1:-1, 1:-1]
    beside_all = beside_all + padded[:, 1:-1, 2:, 1:-1] + padded[:, 1:-1, :-2, 1:-1]
    beside_all = beside_all + padded[:, 1:-1, 1:-1, 2:] + padded[:, 1:-1, 1:-1, :-2]
    return beside_all - 6.0 * centre


def local(positions, velocities, weights, counts, link_offset, link_mask, bin_box, bin_cell, fluid):
    bin_count = positions.shape[1]
    slot_count = positions.shape[2]
    cell_count = fluid.shape[1] * fluid.shape[2] * fluid.shape[3]
    flat_fluid = fluid.reshape(3, cell_count)
    occupied = (
        lax.broadcasted_iota(jnp.int32, (bin_count, slot_count), 1) < counts[:, None]
    ).astype(jnp.float32)
    carried = weights * occupied
    target = bin_box[:, 0]
    box_piece = lax.all_gather(flat_fluid[None], ("gx", "gy"), axis=0, tiled=True)
    first_box = jnp.int32(0)
    local_box = jnp.clip(target, 0, box_piece.shape[0] - 1)
    inside = (target >= first_box) & (target < first_box + box_piece.shape[0])
    picked = box_piece[local_box, :, bin_cell]
    fluid_seen = jnp.where(inside[:, None], picked, 0.0).T
    neighbour = lax.broadcasted_iota(jnp.int32, (bin_count, 1), 0) + link_offset + bin_count
    link_weight = link_mask.astype(jnp.float32)
    block_bins = 16
    state_pos = positions
    state_vel = velocities
    pulled_total = jnp.zeros((3, bin_count), jnp.float32)
    for substep in range(SUBSTEPS):
        packed = jnp.concatenate([state_pos, state_vel, carried[None]], 0)
        widened = padded_2(packed, ((("gx", "gy", "gz"), 1),), bin_count)
        state_pos, state_vel, pulled = advance(
            widened,
            state_pos,
            state_vel,
            carried,
            occupied,
            fluid_seen,
            neighbour,
            link_weight,
            block_bins,
        )
        pulled_total = pulled_total + pulled
    pushed_all = -coupling * pulled_total.T
    first_box = jnp.int32(0)
    local_box = jnp.clip(target, 0, 1 * lax.axis_size(("gx", "gy")) - 1)
    inside = (target >= first_box) & (target < first_box + 1 * lax.axis_size(("gx", "gy")))
    pushed = jnp.where(inside[:, None], pushed_all, 0.0)
    source = lax.psum_scatter(
        jnp.zeros((1 * lax.axis_size(("gx", "gy")), 3, cell_count), jnp.float32)
        .at[local_box, :, bin_cell]
        .add(pushed),
        ("gx", "gy"),
        scatter_dimension=0,
        tiled=True,
    ).reshape(fluid.shape)

    def fluid_rate(velocity_field):
        padded = padded_2(velocity_field, (("gx", 1), ("gy", 2), ("gz", 3)), 1)
        return viscosity * stencil(padded) + source

    first_rate = fluid_rate(fluid)
    middle = fluid + first_rate
    second_rate = fluid_rate(middle)
    fluid_out = fluid + 0.5 * (first_rate + second_rate)
    return (state_pos, state_vel, fluid_out)


def solution(mesh):
    in_specs = (
        P(None, ("gx", "gy", "gz"), None),
        P(None, ("gx", "gy", "gz"), None),
        P(("gx", "gy", "gz"), None),
        P(("gx", "gy", "gz")),
        P(("gx", "gy", "gz"), None),
        P(("gx", "gy", "gz"), None),
        P(("gx", "gy", "gz"), None),
        P(("gx", "gy", "gz")),
        P(None, "gx", "gy", "gz"),
    )
    out_specs = (
        P(None, ("gx", "gy", "gz"), None),
        P(None, ("gx", "gy", "gz"), None),
        P(None, "gx", "gy", "gz"),
    )
    return jax.shard_map(local, mesh=mesh, in_specs=in_specs, out_specs=out_specs, check_vma=False)
```

profile of v0, /device:TPU:1, one launch (start us, length us, event | category | flops | bytes accessed | tf_op | source)
XLA Modules:
  0.0 500.4 jit_solution(973373740408308659)
XLA Ops:
  7.2 0.8 copy.128
  8.0 0.8 copy.127
  8.7 0.8 fusion.94
  9.5 12.0 %collective-permute-start.1 = (f32[7,16,128]{2,0,1:T(8,128)S(1)}, f32[7,16,128]{2,0,1:T(8,128)S(1)}, u32[]{:S(2)}, u32[]{:S(2)}) collective-permute-start(f32[7,16,128]{2,0,1:T(8,128)S(1)} %pad_maximum_fusion.5), channel_id=1, source_target_pairs={{1,0},{2,1},{3,2},{4,3},{5,4},{6,5},{7,6},{8,7},{9,8},{10,9},{11,1... | collective-permute-start | bytes 172040 | tf_op jit(solution)/shard_map/ppermute | solution.py:28
  21.5 1.9 collective-permute-start
  23.4 0.7 fusion.115
  24.2 1.9 collective-permute-start.5
  26.1 2.4 collective-permute-start.4
  28.5 0.8 broadcast_in_dim_reshape.3
  29.3 0.7 slice_bitcast_fusion.2
  30.1 30.5 %all_gather.3 = f32[16,3,4096]{2,1,0:T(4,128)S(1)} all-gather(f32[1,3,4096]{2,1,0:T(4,128)S(1)} %broadcast_in_dim_reshape.3), channel_id=1, replica_groups=mesh['gx'=4,'gy'=4,'gz'=8] {'gx','gy'}, dimensions={0}, use_global_device_ids=true | all-gather | bytes 835584 | tf_op jit(solution)/shard_map/all_gather | solution.py:94
  60.6 15.6 %copy.101 = f32[16,3,4096]{1,2,0:T(8,128)} copy(f32[16,3,4096]{2,1,0:T(4,128)S(1)} %all_gather.3) | data formatting | bytes 1572864 | tf_op jit(solution)/shard_map/all_gather | solution.py:94
  76.2 0.1 copy.94
  76.3 0.1 reshape.48
  76.4 1.3 gather_fusion.1
  77.9 0.6 gather_fusion
  78.7 0.1 pad_maximum_fusion.41
  78.8 2.3 fusion.2
  81.1 5.6 %fusion.49 = f32[3,16,128]{2,0,1:T(4,128)S(1)} fusion(f32[16,4,128]{2,1,0:T(4,128)S(1)} %bitcast.141, f32[16,128]{1,0:T(8,128)S(1)} %get-tuple-element.117, f32[16,4,128]{2,1,0:T(4,128)S(1)} %bitcast.144, f32[16,128]{1,0:T(8,128)S(1)} %get-tuple-element.116, f32[16,4,128]{2,1,0:T(4,128)S(1)} %bitcast.138, f32[16,128]{1,0:T(8,128)S(1)} %get-tuple-element.115, ...), kind=kOutput, calls=%fused_computation.55 | convolution fusion | flops 48277504 | bytes 311296 | tf_op jit(solution)/shard_map/while/body/eval_jaxpr/bqij,cbqj->cbi/dot_general | solution.py:44
  86.7 5.9 %multiply_reduce_fusion = (f32[3,16]{0,1:T(8,128)S(1)}, f32[3,16]{0,1:T(8,128)S(1)}, f32[3,16,128]{2,0,1:T(4,128)S(1)}, f32[3,16,128]{2,0,1:T(4,128)S(1)}) fusion(f32[16,128]{1,0:T(8,128)S(1)} %get-tuple-element.121, f32[3,16]{0,1:T(8,128)S(1)} %select_bitcast_fusion.1, f32[3,16,128]{2,1,0:T(8,128)S(1)} %copy-done.2, ...), kind=kOutput, calls=%fused_computation.141 | convolution fusion | flops 48351136 | bytes 401984 | tf_op jit(solution)/shard_map/while/body/eval_jaxpr/bqij,cbqj->cbi/dot_general | solution.py:45
  92.7 11.0 %broadcast_in_dim.105 = f32[16,3,4096]{1,2,0:T(8,128)} broadcast(f32[]{:T(128)} %constant.18.clone.1), dimensions={} | broadcast | bytes 786436 | tf_op jit(solution)/shard_map/broadcast_in_dim | solution.py:127
  103.8 2.2 scatter_fusion
  106.0 1.3 collective-permute-start.6
  107.3 4.0 collective-permute-start.7
  111.3 0.8 collective-permute-done.7
  112.1 0.1 fusion.112
  112.2 1.3 collective-permute-start.9
  113.5 1.3 collective-permute-start.8
  114.8 17.0 %collective-permute-start.3 = (f32[7,16,128]{2,0,1:T(8,128)S(1)}, f32[7,16,128]{2,0,1:T(8,128)S(1)}, u32[]{:S(2)}, u32[]{:S(2)}) collective-permute-start(f32[7,16,128]{2,0,1:T(8,128)S(1)} %pad_maximum_fusion.4), channel_id=1, source_target_pairs={{1,0},{2,1},{3,2},{4,3},{5,4},{6,5},{7,6},{8,7},{9,8},{10,9},{11,1... | collective-permute-start | bytes 172040 | tf_op jit(solution)/shard_map/ppermute | solution.py:28
  131.8 1.9 collective-permute-start.2
  133.8 10.0 %collective-permute-done.2 = f32[7,16,128]{2,0,1:T(8,128)S(1)} collective-permute-done((f32[7,16,128]{2,0,1:T(8,128)S(1)}, f32[7,16,128]{2,0,1:T(8,128)S(1)}, u32[]{:S(2)}, u32[]{:S(2)}) %collective-permute-start.2) | collective-permute-done | bytes 57376 | tf_op jit(solution)/shard_map/ppermute | solution.py:26
  143.8 0.6 gather_fusion.2
  144.7 315.4 %reduce-scatter.2.cloned.1.call-done = f32[1,3,4096]{1,2,0:T(8,128)} async-done(((f32[16,3,4096]{1,2,0:T(8,128)}), f32[1,3,4096]{1,2,0:T(8,128)}) %reduce-scatter.2.cloned.1.call-update) | async-done | bytes 49168 | tf_op jit(solution)/shard_map/reduce_scatter | solution.py:126
  460.1 2.2 copy.109
  462.3 0.1 fusion.106
  462.5 1.9 collective-permute-start.10
  464.4 3.6 collective-permute-start.11
  468.0 2.2 fusion.5
  470.3 1.3 collective-permute-start.12
  471.6 4.0 collective-permute-start.13
  475.6 5.6 %fusion.57 = f32[3,16,128]{2,0,1:T(4,128)S(1)} fusion(f32[16,4,128]{2,1,0:T(4,128)S(1)} %bitcast.132, f32[16,128]{1,0:T(8,128)S(1)} %bitcast.150, f32[16,4,128]{2,1,0:T(4,128)S(1)} %bitcast.135, f32[16,128]{1,0:T(8,128)S(1)} %bitcast.153, f32[16,4,128]{2,1,0:T(4,128)S(1)} %bitcast.129, f32[16,128]{1,0:T(8,128)S(1)} %bitcast.147, ...), kind=kOutput, calls=%fused_computation.63 | convolution fusion | flops 48277504 | bytes 311296 | tf_op jit(solution)/shard_map/while/body/eval_jaxpr/bqij,cbqj->cbi/dot_general | solution.py:44
  481.3 0.1 fusion.111
  481.4 3.2 collective-permute-start.15
  484.6 1.3 collective-permute-start.14
  485.9 5.6 %multiply_add_fusion = (f32[3,16,128]{2,0,1:T(4,128)S(1)}, f32[3,16,128]{2,0,1:T(4,128)S(1)}) fusion(f32[3,16,128]{2,0,1:T(4,128)S(1)} %get-tuple-element.109, f32[16,128]{1,0:T(8,128)S(1)} %get-tuple-element.120, f32[3,16,128]{2,0,1:T(4,128)S(1)} %get-tuple-element.122, f32[3,16]{0,1:T(8,128)S(1)} %select_bitcast_fusion.1, f32[3,16,128]{2,0,1:T(4,128)S(1)} %fusion.57, ...), kind=kOutput, calls=%fused_computation.143 | convolution fusion | flops 48320512 | bytes 393408 | tf_op jit(solution)/shard_map/while/body/eval_jaxpr/bqij,cbqj->cbi/dot_general | solution.py:45
  491.5 0.6 copy.111
  492.2 0.6 copy.112
  492.8 0.8 fusion.80
  (61 shorter events, 1.0 us)
Async XLA Ops:
  7.2 452.9 %reduce-scatter.2.cloned.1.call-start = ((), (), s32[]{:S(2)}) async-start(), calls=%async_computation.1 | async-start | bytes 35651584 | tf_op jit(solution)/shard_map/reduce_scatter | solution.py:126
  9.5 68.3 %collective-permute-start.1 = (f32[7,16,128]{2,0,1:T(8,128)S(1)}, f32[7,16,128]{2,0,1:T(8,128)S(1)}, u32[]{:S(2)}, u32[]{:S(2)}) collective-permute-start(f32[7,16,128]{2,0,1:T(8,128)S(1)} %pad_maximum_fusion.5), channel_id=1, source_target_pairs={{1,0},{2,1},{3,2},{4,3},{5,4},{6,5},{7,6},{8,7},{9,8},{10,9},{11,1... | collective-permute-start | bytes 172040 | tf_op jit(solution)/shard_map/ppermute | solution.py:28
  21.5 56.4 %collective-permute-start = (f32[7,16,128]{2,0,1:T(8,128)S(1)}, f32[7,16,128]{2,0,1:T(8,128)S(1)}, u32[]{:S(2)}, u32[]{:S(2)}) collective-permute-start(f32[7,16,128]{2,0,1:T(8,128)S(1)} %pad_maximum_fusion.5), channel_id=1, source_target_pairs={{0,1},{1,2},{2,3},{3,4},{4,5},{5,6},{6,7},{7,8},{8,9},{9,10},{10,1... | collective-permute-start | bytes 172040 | tf_op jit(solution)/shard_map/ppermute | solution.py:26
  24.2 53.6 %collective-permute-start.5 = (f32[3,1,8,128]{3,2,1,0:T(8,128)S(1)}, f32[3,1,8,128]{3,2,1,0:T(8,128)S(1)}, u32[]{:S(2)}, u32[]{:S(2)}) collective-permute-start(f32[3,1,8,128]{3,2,1,0:T(8,128)S(1)} %get-tuple-element.108), channel_id=1, source_target_pairs={{0,32},{32,64},{64,96},{1,33},{33,65},{65,97},{2,34},{34,66},{66,9... | collective-permute-start | bytes 36872 | tf_op jit(solution)/shard_map/ppermute | solution.py:26
  26.1 51.8 %collective-permute-start.4 = (f32[3,1,8,128]{3,2,1,0:T(8,128)S(1)}, f32[3,1,8,128]{3,2,1,0:T(8,128)S(1)}, u32[]{:S(2)}, u32[]{:S(2)}) collective-permute-start(f32[3,1,8,128]{3,2,1,0:T(8,128)S(1)} %get-tuple-element.107), channel_id=1, source_target_pairs={{32,0},{64,32},{96,64},{33,1},{65,33},{97,65},{34,2},{66,34},{98,6... | collective-permute-start | bytes 36872 | tf_op jit(solution)/shard_map/ppermute | solution.py:28
  60.6 15.6 %copy-start.6 = (s32[16,1]{0,1:T(1,128)S(1)}, s32[16,1]{0,1:T(1,128)}, u32[]{:S(2)}) copy-start(s32[16,1]{0,1:T(1,128)} %param.15) | copy-start | bytes 196
  60.6 15.6 %copy-start.5 = (s32[16]{0:T(128)S(1)}, s32[16]{0:T(128)}, u32[]{:S(2)}) copy-start(s32[16]{0:T(128)} %param.16) | copy-start | bytes 196
  60.6 15.6 %copy-start.3 = (s32[16,3]{0,1:T(4,128)S(1)}, s32[16,3]{0,1:T(4,128)}, u32[]{:S(2)}) copy-start(s32[16,3]{0,1:T(4,128)} %param.13) | copy-start | bytes 580
  60.6 17.2 %copy-start.4 = (s32[16,3]{0,1:T(4,128)S(1)}, s32[16,3]{0,1:T(4,128)}, u32[]{:S(2)}) copy-start(s32[16,3]{0,1:T(4,128)} %param.14) | copy-start | bytes 580
  60.6 17.2 %copy-start = (f32[3,4,8,128]{3,2,1,0:T(8,128)S(1)}, f32[3,4,8,128]{3,2,1,0:T(8,128)}, u32[]{:S(2)}) copy-start(f32[3,4,8,128]{3,2,1,0:T(8,128)} %param.17) | copy-start | bytes 147460
  60.6 20.5 %copy-start.1 = (f32[3,16,128]{2,1,0:T(8,128)S(1)}, f32[3,16,128]{2,1,0:T(8,128)}, u32[]{:S(2)}) copy-start(f32[3,16,128]{2,1,0:T(8,128)} %param.9) | copy-start | bytes 73732
  81.1 5.6 %copy-start.2 = (f32[3,16,128]{2,1,0:T(8,128)S(1)}, f32[3,16,128]{2,1,0:T(8,128)}, u32[]{:S(2)}) copy-start(f32[3,16,128]{2,1,0:T(8,128)} %param.10) | copy-start | bytes 73732
  106.0 5.3 %collective-permute-start.6 = (f32[3,6,1,128]{3,2,1,0:T(1,128)S(1)}, f32[3,6,1,128]{3,2,1,0:T(1,128)S(1)}, u32[]{:S(2)}, u32[]{:S(2)}) collective-permute-start(f32[3,6,1,128]{3,2,1,0:T(1,128)S(1)} %get-tuple-element.104), channel_id=1, source_target_pairs={{8,0},{16,8},{24,16},{9,1},{17,9},{25,17},{10,2},{18,10},{26,18},{... | collective-permute-start | bytes 27656 | tf_op jit(solution)/shard_map/ppermute | solution.py:28
  107.3 4.8 collective-permute-start.7
  112.2 350.1 %collective-permute-start.9 = (f32[3,6,10,1]{3,2,1,0:T(8,128)S(1)}, f32[3,6,10,1]{3,2,1,0:T(8,128)S(1)}, u32[]{:S(2)}, u32[]{:S(2)}) collective-permute-start(f32[3,6,10,1]{3,2,1,0:T(8,128)S(1)} %get-tuple-element.82), channel_id=1, source_target_pairs={{0,1},{1,2},{2,3},{3,4},{4,5},{5,6},{6,7},{8,9},{9,10},{10,11},{11... | collective-permute-start | bytes 2168 | tf_op jit(solution)/shard_map/ppermute | solution.py:26
  113.5 348.8 %collective-permute-start.8 = (f32[3,6,10,1]{3,2,1,0:T(8,128)S(1)}, f32[3,6,10,1]{3,2,1,0:T(8,128)S(1)}, u32[]{:S(2)}, u32[]{:S(2)}) collective-permute-start(f32[3,6,10,1]{3,2,1,0:T(8,128)S(1)} %get-tuple-element.81), channel_id=1, source_target_pairs={{1,0},{2,1},{3,2},{4,3},{5,4},{6,5},{7,6},{9,8},{10,9},{11,10},{12... | collective-permute-start | bytes 2168 | tf_op jit(solution)/shard_map/ppermute | solution.py:28
  114.8 19.0 %collective-permute-start.3 = (f32[7,16,128]{2,0,1:T(8,128)S(1)}, f32[7,16,128]{2,0,1:T(8,128)S(1)}, u32[]{:S(2)}, u32[]{:S(2)}) collective-permute-start(f32[7,16,128]{2,0,1:T(8,128)S(1)} %pad_maximum_fusion.4), channel_id=1, source_target_pairs={{1,0},{2,1},{3,2},{4,3},{5,4},{6,5},{7,6},{8,7},{9,8},{10,9},{11,1... | collective-permute-start | bytes 172040 | tf_op jit(solution)/shard_map/ppermute | solution.py:28
  131.8 11.9 %collective-permute-start.2 = (f32[7,16,128]{2,0,1:T(8,128)S(1)}, f32[7,16,128]{2,0,1:T(8,128)S(1)}, u32[]{:S(2)}, u32[]{:S(2)}) collective-permute-start(f32[7,16,128]{2,0,1:T(8,128)S(1)} %pad_maximum_fusion.4), channel_id=1, source_target_pairs={{0,1},{1,2},{2,3},{3,4},{4,5},{5,6},{6,7},{7,8},{8,9},{9,10},{10,1... | collective-permute-start | bytes 172040 | tf_op jit(solution)/shard_map/ppermute | solution.py:26
  462.5 7.8 %collective-permute-start.10 = (f32[3,1,8,128]{3,2,1,0:T(8,128)S(1)}, f32[3,1,8,128]{3,2,1,0:T(8,128)S(1)}, u32[]{:S(2)}, u32[]{:S(2)}) collective-permute-start(f32[3,1,8,128]{3,2,1,0:T(8,128)S(1)} %get-tuple-element.106), channel_id=1, source_target_pairs={{32,0},{64,32},{96,64},{33,1},{65,33},{97,65},{34,2},{66,34},{98,6... | collective-permute-start | bytes 36872 | tf_op jit(solution)/shard_map/ppermute | solution.py:28
  464.4 5.9 %collective-permute-start.11 = (f32[3,1,8,128]{3,2,1,0:T(8,128)S(1)}, f32[3,1,8,128]{3,2,1,0:T(8,128)S(1)}, u32[]{:S(2)}, u32[]{:S(2)}) collective-permute-start(f32[3,1,8,128]{3,2,1,0:T(8,128)S(1)} %get-tuple-element.105), channel_id=1, source_target_pairs={{0,32},{32,64},{64,96},{1,33},{33,65},{65,97},{2,34},{34,66},{66,9... | collective-permute-start | bytes 36872 | tf_op jit(solution)/shard_map/ppermute | solution.py:26
  470.3 10.9 %collective-permute-start.12 = (f32[3,6,1,128]{3,2,1,0:T(1,128)S(1)}, f32[3,6,1,128]{3,2,1,0:T(1,128)S(1)}, u32[]{:S(2)}, u32[]{:S(2)}) collective-permute-start(f32[3,6,1,128]{3,2,1,0:T(1,128)S(1)} %get-tuple-element.102), channel_id=1, source_target_pairs={{8,0},{16,8},{24,16},{9,1},{17,9},{25,17},{10,2},{18,10},{26,18},{... | collective-permute-start | bytes 27656 | tf_op jit(solution)/shard_map/ppermute | solution.py:28
  471.6 9.6 %collective-permute-start.13 = (f32[3,6,1,128]{3,2,1,0:T(1,128)S(1)}, f32[3,6,1,128]{3,2,1,0:T(1,128)S(1)}, u32[]{:S(2)}, u32[]{:S(2)}) collective-permute-start(f32[3,6,1,128]{3,2,1,0:T(1,128)S(1)} %get-tuple-element.101), channel_id=1, source_target_pairs={{0,8},{8,16},{16,24},{1,9},{9,17},{17,25},{2,10},{10,18},{18,26},{... | collective-permute-start | bytes 27656 | tf_op jit(solution)/shard_map/ppermute | solution.py:26
  481.4 11.4 %collective-permute-start.15 = (f32[3,6,10,1]{3,2,1,0:T(8,128)S(1)}, f32[3,6,10,1]{3,2,1,0:T(8,128)S(1)}, u32[]{:S(2)}, u32[]{:S(2)}) collective-permute-start(f32[3,6,10,1]{3,2,1,0:T(8,128)S(1)} %get-tuple-element.80), channel_id=1, source_target_pairs={{0,1},{1,2},{2,3},{3,4},{4,5},{5,6},{6,7},{8,9},{9,10},{10,11},{11... | collective-permute-start | bytes 2168 | tf_op jit(solution)/shard_map/ppermute | solution.py:26
  484.6 8.2 %collective-permute-start.14 = (f32[3,6,10,1]{3,2,1,0:T(8,128)S(1)}, f32[3,6,10,1]{3,2,1,0:T(8,128)S(1)}, u32[]{:S(2)}, u32[]{:S(2)}) collective-permute-start(f32[3,6,10,1]{3,2,1,0:T(8,128)S(1)} %get-tuple-element.79), channel_id=1, source_target_pairs={{1,0},{2,1},{3,2},{4,3},{5,4},{6,5},{7,6},{9,8},{10,9},{11,10},{12... | collective-permute-start | bytes 2168 | tf_op jit(solution)/shard_map/ppermute | solution.py:28
Sparse Core Ops, SparseCore 0:
  106.1 353.9 reduce-scatter.1
where the time goes:
time: 505 us; the launch traced here: 500 us
  waiting for transfers between devices  326 us (65%)
  starting transfers between devices  60.4 us (12%)
  local copies, waits for them, and re-layouts  37 us (7%)
  blocking collectives  30.5 us (6%)
  matrix products  22.8 us (5%)
  between operations  14.6 us (3%)
  other arithmetic  9.06 us (2%)
    reduce_scatter x1, waiting for transfers between devices, local(): lax.psum_scatter(jnp.zeros((1 * lax.axis_size(('gx', 'gy')), 3, cell_coun...  315 us
    ppermute x8, starting transfers between devices, padded_2(): lax.ppermute(head, axis, [((i + 1) % count, i) for i in range(ends)])  38.5 us
    all_gather x1, blocking collectives, local(): lax.all_gather(flat_fluid[None], ('gx', 'gy'), axis=0, tiled=True)  30.5 us
    ppermute x8, starting transfers between devices, padded_2(): lax.ppermute(tail, axis, [(i, (i + 1) % count) for i in range(ends)])  21.9 us
    all_gather x1, local copies, waits for them, and re-layouts, local(): lax.all_gather(flat_fluid[None], ('gx', 'gy'), axis=0, tiled=True)  15.6 us
    dot_general x2, matrix products, contact(): pull_vel = jnp.einsum('bqij,cbqj->cbi', kernel, near_vel, precision=highest)  11.6 us
    dot_general x2, matrix products, contact(): pull_pos = jnp.einsum('bqij,cbqj->cbi', kernel, near_pos, precision=highest)  11.2 us
    broadcast_in_dim x1, local copies, waits for them, and re-layouts, local(): jnp.zeros((1 * lax.axis_size(('gx', 'gy')), 3, cell_count), jnp.float32)  11 us
  transfers between devices with their start and end apart: 17, of which 3 were waited for; matrix products, arithmetic and copies ran while one was open for 7% of the time, Pallas kernels for 0%

commit v1 on v0

v1 whole, which is shorter than its diff:
```python
import functools

import jax
import jax.numpy as jnp
from jax import lax
from jax.experimental import pallas as pl
from jax.experimental.pallas import tpu as pltpu
from jax.sharding import PartitionSpec as P

f32, bf16, i32 = jnp.float32, jnp.bfloat16, jnp.int32
MESH = pl.DeviceIdType.MESH
BINS = 16
STEP, STIFF, DAMP, COUPLING, VISC = 0.1, 0.05, 0.05, 0.004, 0.12
ROOT_LOG2E = 1.4426950408889634**0.5


def iota(shape, dim):
    return lax.broadcasted_iota(i32, shape, dim)


def parts(x):
    high = x.astype(bf16).astype(f32)
    rest = x - high
    middle = rest.astype(bf16).astype(f32)
    return high, middle, rest - middle


def stacked(x):
    return jnp.concatenate([p.astype(bf16) for p in parts(x)], axis=0)


def kernel(
    sizes,
    pos,
    vel,
    wts,
    counts,
    loff,
    lmask,
    bbox,
    bcell,
    fluid,
    pos_out,
    vel_out,
    fluid_out,
    wide1,
    wide2,
    own_aug,
    aug,
    vals,
    sums,
    req,
    answer,
    ans,
    dep,
    lane_hot,
    row_hot,
    rate_buf,
    first_buf,
    hx,
    hy,
    hz,
    sy,
    sz,
    halo_send,
    halo_recv,
    group_send,
    group_recv,
    face_send,
    face_recv,
):
    ngx, ngy, ngz = sizes
    group, devices = ngx * ngy, ngx * ngy * ngz
    tiles = -(-group * BINS // 128)
    per_tile = 128 // BINS
    gx, gy, gz = (lax.axis_index(a) for a in ("gx", "gy", "gz"))
    me = gx * ngy + gy
    here = me * ngz + gz

    def in_group(g):
        return (lax.div(g, ngy), lax.rem(g, ngy), gz)

    def at(n):
        g = lax.div(n, ngz)
        return (lax.div(g, ngy), lax.rem(g, ngy), lax.rem(n, ngz))

    bin_right, bin_left = at(lax.rem(here + 1, devices)), at(lax.rem(here + devices - 1, devices))
    faces = (
        (lax.rem(gx + 1, ngx), gy, gz),
        (lax.rem(gx + ngx - 1, ngx), gy, gz),
        (gx, lax.rem(gy + 1, ngy), gz),
        (gx, lax.rem(gy + ngy - 1, ngy), gz),
        (gx, gy, lax.rem(gz + 1, ngz)),
        (gx, gy, lax.rem(gz + ngz - 1, ngz)),
    )

    barrier = pltpu.get_barrier_semaphore()

    @pl.loop(1, group)
    def _(k):
        pl.semaphore_signal(
            barrier, inc=1, device_id=in_group(lax.rem(me + k, group)), device_id_type=MESH
        )

    for other in (bin_right, bin_left, faces[4], faces[5]):
        pl.semaphore_signal(barrier, inc=1, device_id=other, device_id_type=MESH)

    row8, lane8 = iota((8, 128), 0), iota((8, 128), 1)
    row16, lane16 = iota((16, 128), 0), iota((16, 128), 1)

    for c in range(3):
        wide1[BINS : 2 * BINS, c, :] = pos[c]
        wide1[BINS : 2 * BINS, 3 + c, :] = vel[c]
    count_rows = jnp.zeros((16, 128), i32)
    asked = jnp.zeros((8, 128), i32)
    first_lane = lax.rem(me, per_tile) * BINS
    for b in range(BINS):
        count_rows = jnp.where(row16 == b, counts[b], count_rows)
        asked = jnp.where(
            lane8 == first_lane + b,
            jnp.where(row8 == 0, bbox[b, 0], jnp.where(row8 == 1, bcell[b], 0)),
            asked,
        )
    occupied = jnp.where(lane16 < count_rows, 1.0, 0.0).astype(f32)
    wide1[BINS : 2 * BINS, 6, :] = wts[...] * occupied
    wide1[BINS : 2 * BINS, 7, :] = occupied
    req[me] = asked

    def face_sources(turn, field):
        for side, (edge_row, edge_lane) in enumerate(((7, 127), (0, 0))):
            rows, lanes = jnp.zeros((16, 128), f32), jnp.zeros((8, 128), f32)
            for c in range(3):
                for x in range(4):
                    k = c * 4 + x
                    tile = field[c, x]
                    rows = jnp.where(row16 == k, tile[edge_row : edge_row + 1, :], rows)
                    lanes = jnp.where(lane8 == k, tile[:, edge_lane : edge_lane + 1], lanes)
            sy[turn, side] = rows
            sz[turn, side] = lanes

    def face_copies(turn, field):
        pairs = (
            (field.at[:, 3], hx.at[turn, 0]),
            (field.at[:, 0], hx.at[turn, 1]),
            (sy.at[turn, 0], hy.at[turn, 0]),
            (sy.at[turn, 1], hy.at[turn, 1]),
            (sz.at[turn, 0], hz.at[turn, 0]),
            (sz.at[turn, 1], hz.at[turn, 1]),
        )
        return [
            pltpu.make_async_remote_copy(
                src_ref=src,
                dst_ref=dst,
                send_sem=face_send.at[turn, n],
                recv_sem=face_recv.at[turn, n],
                device_id=faces[n],
                device_id_type=MESH,
            )
            for n, (src, dst) in enumerate(pairs)
        ]

    def halo_copies(turn, wide):
        own = wide.at[pl.ds(BINS, BINS)]
        return [
            pltpu.make_async_remote_copy(
                src_ref=own,
                dst_ref=wide.at[pl.ds(start, BINS)],
                send_sem=halo_send.at[turn, n],
                recv_sem=halo_recv.at[turn, n],
                device_id=other,
                device_id_type=MESH,
            )
            for n, (start, other) in enumerate(((0, bin_right), (2 * BINS, bin_left)))
        ]

    def group_copy(turn, src, dst, other):
        return pltpu.make_async_remote_copy(
            src_ref=src,
            dst_ref=dst,
            send_sem=group_send.at[turn],
            recv_sem=group_recv.at[turn],
            device_id=other,
            device_id_type=MESH,
        )

    def group_start(turn, buffer, source):
        @pl.loop(1, group)
        def _(k):
            other = lax.rem(me + k, group)
            group_copy(turn, source(other), buffer.at[me], in_group(other)).start()

    def group_all(turn, buffer):
        most = buffer.at[pl.ds(0, group - 1)]
        return group_copy(turn, most, most, in_group(lax.rem(me + 1, group)))

    def gathered(buffer):
        out = []
        for t in range(tiles):
            total = buffer[t * per_tile]
            for s in range(t * per_tile + 1, min(group, (t + 1) * per_tile)):
                total = total + buffer[s]
            out.append(total)
        return jnp.concatenate(out, axis=1) if tiles > 1 else out[0]

    face_sources(0, fluid)
    pl.semaphore_wait(barrier, group - 1 + 4)

    group_start(0, req, lambda other: req.at[me])
    halo1 = halo_copies(0, wide1)
    for copy in halo1:
        copy.start()
    faces0 = face_copies(0, fluid)
    for copy in faces0:
        copy.start()

    def prepare(wide, slot, scale, own):
        tile = wide[slot]
        carried = tile[6:7, :] * scale
        v = jnp.where(row8 < 6, tile, jnp.where(row8 == 6, 1.0, 0.0)) * carried
        vh, vm, vl = parts(v)
        vals[slot] = jnp.concatenate([vh, vm, vl, jnp.zeros_like(vh)], axis=0).astype(bf16)
        y = jnp.where(row8 < 3, tile * ROOT_LOG2E, 0.0)
        norm = -0.5 * jnp.sum(y * y, axis=0, keepdims=True)
        h, m, l = parts(jnp.where(row8 == 3, norm, y))
        ones = jnp.where((row8 >= 4) & (row8 < 7), 1.0, h)
        aug[slot] = jnp.concatenate([ones, m, l, h, m, h], axis=0).astype(bf16)
        if own:
            high = jnp.where(row8 < 3, h, jnp.where(row8 == 3, 1.0, 0.0))
            low = jnp.where(row8 < 3, m, 0.0)
            lowest = jnp.where(row8 < 3, l, 0.0)
            norms = jnp.where(
                row8 == 4,
                h[3:4, :],
                jnp.where(row8 == 5, m[3:4, :], jnp.where(row8 == 6, l[3:4, :], high)),
            )
            own_aug[slot - BINS] = jnp.concatenate(
                [norms, high, high, low, low, lowest], axis=0
            ).astype(bf16)

    def prepare_own(wide):
        @pl.loop(BINS, 2 * BINS)
        def _(slot):
            prepare(wide, slot, 1.0, True)

    has_left = jnp.where(here > 0, 1.0, 0.0).astype(f32)
    has_right = jnp.where(here < devices - 1, 1.0, 0.0).astype(f32)

    def prepare_halo(wide):
        @pl.loop(0, BINS)
        def _(slot):
            prepare(wide, slot, has_left, False)
            prepare(wide, slot + 2 * BINS, has_right, False)

    def contact(b):
        slots = [b + BINS]
        for q in range(3):
            slots.append(jnp.where(lmask[b, q] != 0, b + BINS + loff[b, q], 3 * BINS))
        near = jnp.concatenate([aug[s] for s in slots], axis=1)
        value = jnp.concatenate([vals[s] for s in slots], axis=1)
        exponent = lax.dot_general(
            own_aug[b], near, (((0,), (0,)), ((), ())), preferred_element_type=f32
        )
        pair = jnp.exp2(exponent)
        high = pair.astype(bf16)
        low = (pair - high.astype(f32)).astype(bf16)
        by_pair = (((1,), (1,)), ((), ()))
        total = lax.dot_general(value, high, by_pair, preferred_element_type=f32)
        total = total + lax.dot_general(value, low, by_pair, preferred_element_type=f32)
        return total[0:8] + total[8:16] + total[16:24]

    def advanced(tile, total, seen):
        net = tile * total[6:7, :] - total
        force = STIFF * pltpu.roll(net, 3, 0) - DAMP * net
        held = STEP * tile[7:8, :]
        new_v = tile + held * (force + (seen - tile))
        new_x = tile + held * pltpu.roll(new_v, 5, 0)
        return jnp.where(row8 < 3, new_x, jnp.where(row8 < 6, new_v, tile))

    aug[3 * BINS] = jnp.zeros((48, 128), bf16)
    vals[3 * BINS] = jnp.zeros((32, 128), bf16)
    prepare_own(wide1)

    group_all(0, req).wait_recv()
    asked_all = gathered(req)
    wide_lanes = 128 * tiles
    cell = asked_all[1:2, :]
    lane_hot[...] = jnp.where(
        iota((128, wide_lanes), 0) == (cell & 127), 1.0, 0.0
    ).astype(bf16)
    row_hot[...] = jnp.where(
        (iota((32, wide_lanes), 0) == (cell >> 7)) & (asked_all[0:1, :] == me), 1.0, 0.0
    ).astype(f32)
    at_lane = jnp.dot(
        stacked(fluid[...].reshape(96, 128)), lane_hot[...], preferred_element_type=f32
    )
    at_lane = at_lane[0:96] + at_lane[96:192] + at_lane[192:288]
    reply = jnp.zeros((8, wide_lanes), f32)
    wide_row = iota((8, wide_lanes), 0)
    for c in range(3):
        picked = jnp.sum(at_lane[32 * c : 32 * c + 32] * row_hot[...], axis=0, keepdims=True)
        reply = jnp.where(wide_row == 3 + c, picked, reply)
    for t in range(tiles):
        answer[t] = reply[:, 128 * t : 128 * t + 128]
    ans[me] = answer[lax.div(me, per_tile)]
    group_start(1, ans, lambda other: answer.at[lax.div(other, per_tile)])

    in_x = [jnp.where(g, 1.0, 0.0).astype(f32) for g in (gx > 0, gx < ngx - 1)]
    in_y = [jnp.where(g, 1.0, 0.0).astype(f32) for g in (gy > 0, gy < ngy - 1)]
    in_z = [jnp.where(g, 1.0, 0.0).astype(f32) for g in (gz > 0, gz < ngz - 1)]

    def laplace(turn, field, c, x):
        k = c * 4 + x
        tile = field[c, x]
        below = field[c, x - 1] if x > 0 else hx[turn, 0, c] * in_x[0]
        above = field[c, x + 1] if x < 3 else hx[turn, 1, c] * in_x[1]
        total = below + above - 6.0 * tile
        total = total + jnp.where(
            row8 == 0, hy[turn, 0, k : k + 1, :] * in_y[0], pltpu.roll(tile, 1, 0)
        )
        total = total + jnp.where(
            row8 == 7, hy[turn, 1, k : k + 1, :] * in_y[1], pltpu.roll(tile, 7, 0)
        )
        zl, zr = hz[turn, 0] * in_z[0], hz[turn, 1] * in_z[1]
        total = total + jnp.where(lane8 == 0, zl[:, k : k + 1], pltpu.roll(tile, 1, 1))
        return total + jnp.where(lane8 == 127, zr[:, k : k + 1], pltpu.roll(tile, 127, 1))

    for copy in faces0:
        copy.wait_recv()
    for c in range(3):
        for x in range(4):
            rate_buf[c, x] = VISC * laplace(0, fluid, c, x)

    for copy in halo1:
        copy.wait_recv()
    prepare_halo(wide1)

    @pl.loop(0, BINS, unroll=4)
    def _(b):
        sums[b] = contact(b)

    group_all(1, ans).wait_recv()
    seen = ans[0]
    for s in range(1, group):
        seen = seen + ans[s]
    seen = pltpu.roll(seen, lax.rem(128 - first_lane, 128), 1)
    drawn = jnp.zeros((8, 128), f32)
    for b in range(BINS):
        seen_b = jnp.broadcast_to(seen[:, b : b + 1], (8, 128))
        tile = wide1[BINS + b]
        new = advanced(tile, sums[b], seen_b)
        wide2[BINS + b] = new
        drag = (seen_b - tile) + (seen_b - new)
        pulled = jnp.sum(tile[6:7, :] * drag, axis=1, keepdims=True)
        drawn = jnp.where(lane8 == b, pulled, drawn)
    dep[me] = pltpu.roll(drawn, first_lane, 1)
    halo2 = halo_copies(1, wide2)
    for copy in halo2:
        copy.start()
    group_start(2, dep, lambda other: dep.at[me])
    prepare_own(wide2)

    group_all(2, dep).wait_recv()
    pushed = -COUPLING * gathered(dep)
    spread = jnp.concatenate(
        [pushed[3 + c : 4 + c, :] * row_hot[...] for c in range(3)], axis=0
    )
    source = lax.dot_general(
        stacked(spread), lane_hot[...], (((1,), (1,)), ((), ())), preferred_element_type=f32
    )
    source = source[0:96] + source[96:192] + source[192:288]
    first_buf[...] = rate_buf[...] + source.reshape(3, 4, 8, 128)
    face_sources(1, first_buf)
    faces1 = face_copies(1, first_buf)
    for copy in faces1:
        copy.start()

    for copy in halo2:
        copy.wait_recv()
    prepare_halo(wide2)

    @pl.loop(0, BINS, unroll=4)
    def _(b):
        sums[b] = contact(b)

    for b in range(BINS):
        sums[b] = advanced(
            wide2[BINS + b], sums[b], jnp.broadcast_to(seen[:, b : b + 1], (8, 128))
        )
    for c in range(3):
        pos_out[c] = sums[:, c, :]
        vel_out[c] = sums[:, 3 + c, :]

    for copy in faces1:
        copy.wait_recv()
    for c in range(3):
        for x in range(4):
            fluid_out[c, x] = (
                fluid[c, x] + first_buf[c, x] + (0.5 * VISC) * laplace(1, first_buf, c, x)
            )

    for copy in (*halo1, *faces0, *halo2, *faces1):
        copy.wait_send()
    for turn, buffer in enumerate((req, ans, dep)):
        group_all(turn, buffer).wait_send()


def local(sizes, *args):
    group = sizes[0] * sizes[1]
    tiles = -(-group * BINS // 128)
    vmem, smem = pl.BlockSpec(memory_space=pltpu.VMEM), pl.BlockSpec(memory_space=pltpu.SMEM)
    dma = pltpu.SemaphoreType.DMA
    return tuple(
        pl.pallas_call(
            functools.partial(kernel, sizes),
            out_shape=(
                jax.ShapeDtypeStruct((3, BINS, 128), f32),
                jax.ShapeDtypeStruct((3, BINS, 128), f32),
                jax.ShapeDtypeStruct((3, 4, 8, 128), f32),
            ),
            in_specs=[vmem] * 3 + [smem] * 5 + [vmem],
            out_specs=(vmem,) * 3,
            scratch_shapes=[
                pltpu.VMEM((3 * BINS, 8, 128), f32),
                pltpu.VMEM((3 * BINS, 8, 128), f32),
                pltpu.VMEM((BINS, 48, 128), bf16),
                pltpu.VMEM((3 * BINS + 1, 48, 128), bf16),
                pltpu.VMEM((3 * BINS + 1, 32, 128), bf16),
                pltpu.VMEM((BINS, 8, 128), f32),
                pltpu.VMEM((group, 8, 128), i32),
                pltpu.VMEM((tiles, 8, 128), f32),
                pltpu.VMEM((group, 8, 128), f32),
                pltpu.VMEM((group, 8, 128), f32),
                pltpu.VMEM((128, 128 * tiles), bf16),
                pltpu.VMEM((32, 128 * tiles), f32),
                pltpu.VMEM((3, 4, 8, 128), f32),
                pltpu.VMEM((3, 4, 8, 128), f32),
                pltpu.VMEM((2, 2, 3, 8, 128), f32),
                pltpu.VMEM((2, 2, 16, 128), f32),
                pltpu.VMEM((2, 2, 8, 128), f32),
                pltpu.VMEM((2, 2, 16, 128), f32),
                pltpu.VMEM((2, 2, 8, 128), f32),
                dma((2, 2)),
                dma((2, 2)),
                dma((3,)),
                dma((3,)),
                dma((2, 6)),
                dma((2, 6)),
            ],
            compiler_params=pltpu.CompilerParams(
                collective_id=0, has_side_effects=True, vmem_limit_bytes=16 * 2**20
            ),
            name="bed_step",
        )(*args)
    )


def solution(mesh):
    sizes = tuple(mesh.shape[a] for a in ("gx", "gy", "gz"))
    bins = ("gx", "gy", "gz")
    in_specs = (
        P(None, bins, None),
        P(None, bins, None),
        P(bins, None),
        P(bins),
        P(bins, None),
        P(bins, None),
        P(bins, None),
        P(bins),
        P(None, "gx", "gy", "gz"),
    )
    out_specs = (P(None, bins, None), P(None, bins, None), P(None, "gx", "gy", "gz"))
    return jax.shard_map(
        functools.partial(local, sizes),
        mesh=mesh,
        in_specs=in_specs,
        out_specs=out_specs,
        check_vma=False,
    )
```

time: 505 us -> 38.1 us (0.08)
  waiting for transfers between devices: 326 us -> 0 us
  starting transfers between devices: 60.4 us -> 0 us
  Pallas kernels: 0 us -> 31.4 us
  local copies, waits for them, and re-layouts: 37 us -> 5.69 us
  blocking collectives: 30.5 us -> 0 us
  matrix products: 22.8 us -> 0 us
  between operations: 14.6 us -> 0.67 us
  other arithmetic: 9.06 us -> 0 us
    reduce_scatter x1 -> x0, waiting for transfers between devices: 315 us -> none  [local(): lax.psum_scatter(jnp.zeros((1 * lax.axis_size(('gx', 'gy')), 3, cell_coun...]
    ppermute x16 -> x0, starting transfers between devices: 60.3 us -> none  [the longest x8 38.5 us: padded_2(): lax.ppermute(head, axis, [((i + 1) % count, i) for i in range(ends)])]
    pallas_call x0 -> x1, Pallas kernels: none -> 31.4 us  [local(): pl.pallas_call(functools.partial(kernel, sizes), out_shape=(jax.ShapeDtyp...]
    all_gather x1 -> x0, blocking collectives: 30.5 us -> none  [local(): lax.all_gather(flat_fluid[None], ('gx', 'gy'), axis=0, tiled=True)]
    dot_general x4 -> x0, matrix products: 22.8 us -> none  [the longest x2 11.6 us: contact(): pull_vel = jnp.einsum('bqij,cbqj->cbi', kernel, near_vel, precision=highest)]
    all_gather x1 -> x0, local copies, waits for them, and re-layouts: 15.6 us -> none  [local(): lax.all_gather(flat_fluid[None], ('gx', 'gy'), axis=0, tiled=True)]
    broadcast_in_dim x2 -> x0, local copies, waits for them, and re-layouts: 11.1 us -> none  [the longest x1 11 us: local(): jnp.zeros((1 * lax.axis_size(('gx', 'gy')), 3, cell_count), jnp.float32)]
    ppermute x16 -> x0, waiting for transfers between devices: 10.8 us -> none  [the longest x8 10.8 us: padded_2(): lax.ppermute(tail, axis, [(i, (i + 1) % count) for i in range(ends)])]
  transfers between devices with their start and end apart: 17 -> 0, of which waited for: 3 -> 0; matrix products, arithmetic and copies ran while one was open for 7% -> 0% of each run, Pallas kernels for 0% -> 0%
where the time goes in v1:
time: 38.1 us; the launch traced here: 37.7 us
  Pallas kernels  31.4 us (82%)
  local copies, waits for them, and re-layouts  5.69 us (15%)
  between operations  0.67 us (2%)
    pallas_call x1, Pallas kernels, local(): pl.pallas_call(functools.partial(kernel, sizes), out_shape=(jax.ShapeDtyp...  31.4 us
    unnamed x20, local copies, waits for them, and re-layouts  5.69 us

profile of v1, /device:TPU:1, one launch (start us, length us, event | category | flops | bytes accessed | tf_op | source)
XLA Modules:
  0.0 37.7 jit_solution(16516459538922262957)
XLA Ops:
  0.6 0.0 copy-start.6
  0.6 0.0 copy-start.1
  0.7 0.8 %copy.12.loff = s32[16,3]{1,0:T(8,128)S(1)} copy(s32[16,3]{0,1:T(4,128)} %param.13) | data formatting | bytes 384 | tf_op args[4]
  1.4 0.0 copy-done.6
  1.4 0.1 copy.13.lmask
  1.5 0.0 copy-start.4
  1.5 0.0 copy-start.5
  1.5 0.8 %copy.14.bbox = s32[16,1]{1,0:T(8,128)S(1)} copy(s32[16,1]{0,1:T(1,128)} %param.15) | data formatting | bytes 128 | tf_op args[6]
  2.3 0.0 copy-done.1
  2.3 0.0 copy-done.4
  2.3 0.0 copy-done.5
  2.3 0.0 copy-start
  2.3 0.8 %copy-done = f32[3,4,8,128]{3,2,1,0:T(8,128)S(1)} copy-done((f32[3,4,8,128]{3,2,1,0:T(8,128)S(1)}, f32[3,4,8,128]{3,2,1,0:T(8,128)}, u32[]{:S(2)}) %copy-start) | copy-done | bytes 49176
  3.1 0.0 copy-start.2
  3.1 0.7 %copy-done.2 = f32[3,16,128]{2,1,0:T(8,128)S(1)} copy-done((f32[3,16,128]{2,1,0:T(8,128)S(1)}, f32[3,16,128]{2,1,0:T(8,128)}, u32[]{:S(2)}) %copy-start.2) | copy-done | bytes 24600
  3.8 0.0 copy-start.3
  3.8 0.7 %copy-done.3 = f32[16,128]{1,0:T(8,128)S(1)} copy-done((f32[16,128]{1,0:T(8,128)S(1)}, f32[16,128]{1,0:T(8,128)}, u32[]{:S(2)}) %copy-start.3) | copy-done | bytes 8216
  4.5 31.4 %bed_step.1 = (f32[3,16,128]{2,1,0:T(8,128)S(1)}, f32[3,16,128]{2,1,0:T(8,128)S(1)}, f32[3,4,8,128]{3,2,1,0:T(8,128)S(1)}) custom-call(f32[3,16,128]{2,1,0:T(8,128)S(1)} %copy-done.1, f32[3,16,128]{2,1,0:T(8,128)S(1)} %copy-done.2, f32[16,128]{1,0:T(8,128)S(1)} %copy-done.3, s32[16]{0:T(128)S(1)} %copy-done.4, s32[16,3]{1,0:T(8,128)S(1)} %copy.12.loff, ...), custom_call_target="tpu_custom_call" | custom-call | tf_op jit(solution)/shard_map/bed_step/pallas_call | solution.py:413
  35.9 0.6 %copy.18 = f32[3,16,128]{2,1,0:T(8,128)} copy(f32[3,16,128]{2,1,0:T(8,128)S(1)} %get-tuple-element.6) | data formatting | bytes 49152
  36.5 0.6 %copy.19 = f32[3,16,128]{2,1,0:T(8,128)} copy(f32[3,16,128]{2,1,0:T(8,128)S(1)} %get-tuple-element.7) | data formatting | bytes 49152
  37.1 0.6 %copy.20 = f32[3,4,8,128]{3,2,1,0:T(8,128)} copy(f32[3,4,8,128]{3,2,1,0:T(8,128)S(1)} %get-tuple-element.8) | data formatting | bytes 98304
Async XLA Ops:
  0.6 0.8 %copy-start.6 = (s32[16,3]{0,1:T(4,128)S(1)}, s32[16,3]{0,1:T(4,128)}, u32[]{:S(2)}) copy-start(s32[16,3]{0,1:T(4,128)} %param.14) | copy-start | bytes 580
  0.6 1.6 %copy-start.1 = (f32[3,16,128]{2,1,0:T(8,128)S(1)}, f32[3,16,128]{2,1,0:T(8,128)}, u32[]{:S(2)}) copy-start(f32[3,16,128]{2,1,0:T(8,128)} %pos.1) | copy-start | bytes 73732
  1.5 0.8 %copy-start.4 = (s32[16]{0:T(128)S(1)}, s32[16]{0:T(128)}, u32[]{:S(2)}) copy-start(s32[16]{0:T(128)} %counts.1) | copy-start | bytes 196
  1.5 0.8 %copy-start.5 = (s32[16]{0:T(128)S(1)}, s32[16]{0:T(128)}, u32[]{:S(2)}) copy-start(s32[16]{0:T(128)} %bcell.1) | copy-start | bytes 196
  2.3 0.8 %copy-start = (f32[3,4,8,128]{3,2,1,0:T(8,128)S(1)}, f32[3,4,8,128]{3,2,1,0:T(8,128)}, u32[]{:S(2)}) copy-start(f32[3,4,8,128]{3,2,1,0:T(8,128)} %fluid.1) | copy-start | bytes 147460
  3.1 0.7 %copy-start.2 = (f32[3,16,128]{2,1,0:T(8,128)S(1)}, f32[3,16,128]{2,1,0:T(8,128)}, u32[]{:S(2)}) copy-start(f32[3,16,128]{2,1,0:T(8,128)} %vel.1) | copy-start | bytes 73732
  3.8 0.7 %copy-start.3 = (f32[16,128]{1,0:T(8,128)S(1)}, f32[16,128]{1,0:T(8,128)}, u32[]{:S(2)}) copy-start(f32[16,128]{1,0:T(8,128)} %wts.1) | copy-start | bytes 24580

commit v2 on v1

--- a/solution.py
+++ b/solution.py
@@ -31,6 +31,18 @@
 
 def kernel(
     sizes,
+    pos_in,
+    vel_in,
+    wts_in,
+    counts_in,
+    loff_in,
+    lmask_in,
+    bbox_in,
+    bcell_in,
+    fluid_in,
+    pos_out,
+    vel_out,
+    fluid_out,
     pos,
     vel,
     wts,
@@ -40,9 +52,6 @@
     bbox,
     bcell,
     fluid,
-    pos_out,
-    vel_out,
-    fluid_out,
     wide1,
     wide2,
     own_aug,
@@ -62,6 +71,7 @@
     hz,
     sy,
     sz,
+    load_sem,
     halo_send,
     halo_recv,
     group_send,
@@ -94,6 +104,25 @@
         (gx, gy, lax.rem(gz + ngz - 1, ngz)),
     )
 
+    loads = [
+        pltpu.make_async_copy(src, dst, load_sem.at[n])
+        for n, (src, dst) in enumerate(
+            (
+                (bbox_in, bbox),
+                (bcell_in, bcell),
+                (fluid_in, fluid),
+                (pos_in, pos),
+                (vel_in, vel),
+                (counts_in, counts),
+                (wts_in, wts),
+                (loff_in, loff),
+                (lmask_in, lmask),
+            )
+        )
+    ]
+    for copy in loads:
+        copy.start()
+
     barrier = pltpu.get_barrier_semaphore()
 
     @pl.loop(1, group)
@@ -108,22 +137,16 @@
     row8, lane8 = iota((8, 128), 0), iota((8, 128), 1)
     row16, lane16 = iota((16, 128), 0), iota((16, 128), 1)
 
-    for c in range(3):
-        wide1[BINS : 2 * BINS, c, :] = pos[c]
-        wide1[BINS : 2 * BINS, 3 + c, :] = vel[c]
-    count_rows = jnp.zeros((16, 128), i32)
+    loads[0].wait()
+    loads[1].wait()
     asked = jnp.zeros((8, 128), i32)
     first_lane = lax.rem(me, per_tile) * BINS
     for b in range(BINS):
-        count_rows = jnp.where(row16 == b, counts[b], count_rows)
         asked = jnp.where(
             lane8 == first_lane + b,
-            jnp.where(row8 == 0, bbox[b, 0], jnp.where(row8 == 1, bcell[b], 0)),
+            jnp.where(row8 == 0, bbox[0, b], jnp.where(row8 == 1, bcell[b], 0)),
             asked,
         )
-    occupied = jnp.where(lane16 < count_rows, 1.0, 0.0).astype(f32)
-    wide1[BINS : 2 * BINS, 6, :] = wts[...] * occupied
-    wide1[BINS : 2 * BINS, 7, :] = occupied
     req[me] = asked
 
     def face_sources(turn, field):
@@ -202,7 +225,21 @@
             out.append(total)
         return jnp.concatenate(out, axis=1) if tiles > 1 else out[0]
 
+    loads[2].wait()
     face_sources(0, fluid)
+
+    for copy in loads[3:]:
+        copy.wait()
+    for c in range(3):
+        wide1[BINS : 2 * BINS, c, :] = pos[c]
+        wide1[BINS : 2 * BINS, 3 + c, :] = vel[c]
+    count_rows = jnp.zeros((16, 128), i32)
+    for b in range(BINS):
+        count_rows = jnp.where(row16 == b, counts[b], count_rows)
+    occupied = jnp.where(lane16 < count_rows, 1.0, 0.0).astype(f32)
+    wide1[BINS : 2 * BINS, 6, :] = wts[...] * occupied
+    wide1[BINS : 2 * BINS, 7, :] = occupied
+
     pl.semaphore_wait(barrier, group - 1 + 4)
 
     group_start(0, req, lambda other: req.at[me])
@@ -254,18 +291,17 @@
     def contact(b):
         slots = [b + BINS]
         for q in range(3):
-            slots.append(jnp.where(lmask[b, q] != 0, b + BINS + loff[b, q], 3 * BINS))
+            slots.append(jnp.where(lmask[q, b] != 0, b + BINS + loff[q, b], 3 * BINS))
         near = jnp.concatenate([aug[s] for s in slots], axis=1)
         value = jnp.concatenate([vals[s] for s in slots], axis=1)
         exponent = lax.dot_general(
-            own_aug[b], near, (((0,), (0,)), ((), ())), preferred_element_type=f32
+            near, own_aug[b], (((0,), (0,)), ((), ())), preferred_element_type=f32
         )
         pair = jnp.exp2(exponent)
         high = pair.astype(bf16)
         low = (pair - high.astype(f32)).astype(bf16)
-        by_pair = (((1,), (1,)), ((), ()))
-        total = lax.dot_general(value, high, by_pair, preferred_element_type=f32)
-        total = total + lax.dot_general(value, low, by_pair, preferred_element_type=f32)
+        total = jnp.dot(value, high, preferred_element_type=f32)
+        total = total + jnp.dot(value, low, preferred_element_type=f32)
         return total[0:8] + total[8:16] + total[16:24]
 
     def advanced(tile, total, seen):
@@ -334,7 +370,7 @@
         copy.wait_recv()
     prepare_halo(wide1)
 
-    @pl.loop(0, BINS, unroll=4)
+    @pl.loop(0, BINS, unroll=8)
     def _(b):
         sums[b] = contact(b)
 
@@ -378,7 +414,7 @@
         copy.wait_recv()
     prepare_halo(wide2)
 
-    @pl.loop(0, BINS, unroll=4)
+    @pl.loop(0, BINS, unroll=8)
     def _(b):
         sums[b] = contact(b)
 
@@ -404,22 +440,40 @@
         group_all(turn, buffer).wait_send()
 
 
-def local(sizes, *args):
+def write_out(*refs):
+    sems = refs[-1]
+    copies = [pltpu.make_async_copy(refs[n], refs[3 + n], sems.at[n]) for n in range(3)]
+    for copy in copies:
+        copy.start()
+    for copy in copies:
+        copy.wait()
+
+
+def local(sizes, pos, vel, wts, counts, loff, lmask, bbox, bcell, fluid):
     group = sizes[0] * sizes[1]
     tiles = -(-group * BINS // 128)
-    vmem, smem = pl.BlockSpec(memory_space=pltpu.VMEM), pl.BlockSpec(memory_space=pltpu.SMEM)
+    vmem, anywhere = pl.BlockSpec(memory_space=pltpu.VMEM), pl.BlockSpec(memory_space=pltpu.HBM)
     dma = pltpu.SemaphoreType.DMA
-    return tuple(
-        pl.pallas_call(
+    out_shape = (
+        jax.ShapeDtypeStruct((3, BINS, 128), f32),
+        jax.ShapeDtypeStruct((3, BINS, 128), f32),
+        jax.ShapeDtypeStruct((3, 4, 8, 128), f32),
+    )
+    results = pl.pallas_call(
             functools.partial(kernel, sizes),
-            out_shape=(
-                jax.ShapeDtypeStruct((3, BINS, 128), f32),
-                jax.ShapeDtypeStruct((3, BINS, 128), f32),
-                jax.ShapeDtypeStruct((3, 4, 8, 128), f32),
-            ),
-            in_specs=[vmem] * 3 + [smem] * 5 + [vmem],
+            out_shape=out_shape,
+            in_specs=[anywhere] * 9,
             out_specs=(vmem,) * 3,
             scratch_shapes=[
+                pltpu.VMEM((3, BINS, 128), f32),
+                pltpu.VMEM((3, BINS, 128), f32),
+                pltpu.VMEM((BINS, 128), f32),
+                pltpu.SMEM((BINS,), i32),
+                pltpu.SMEM((3, BINS), i32),
+                pltpu.SMEM((3, BINS), i32),
+                pltpu.SMEM((1, BINS), i32),
+                pltpu.SMEM((BINS,), i32),
+                pltpu.VMEM((3, 4, 8, 128), f32),
                 pltpu.VMEM((3 * BINS, 8, 128), f32),
                 pltpu.VMEM((3 * BINS, 8, 128), f32),
                 pltpu.VMEM((BINS, 48, 128), bf16),
@@ -439,6 +493,7 @@
                 pltpu.VMEM((2, 2, 8, 128), f32),
                 pltpu.VMEM((2, 2, 16, 128), f32),
                 pltpu.VMEM((2, 2, 8, 128), f32),
+                dma((9,)),
                 dma((2, 2)),
                 dma((2, 2)),
                 dma((3,)),
@@ -447,11 +502,18 @@
                 dma((2, 6)),
             ],
             compiler_params=pltpu.CompilerParams(
-                collective_id=0, has_side_effects=True, vmem_limit_bytes=16 * 2**20
+                collective_id=0, has_side_effects=True, vmem_limit_bytes=60 * 2**20
             ),
             name="bed_step",
-        )(*args)
-    )
+        )(pos, vel, wts, counts, loff.T, lmask.T, bbox.T, bcell, fluid)
+    return tuple(pl.pallas_call(
+        write_out,
+        out_shape=out_shape,
+        in_specs=[vmem] * 3,
+        out_specs=(anywhere,) * 3,
+        scratch_shapes=[dma((3,))],
+        name="out_write",
+    )(*results))
 
 
 def solution(mesh):

time: 38.1 us -> 31.1 us (0.82)
  local copies, waits for them, and re-layouts: 5.69 us -> 0 us
  Pallas kernels: 31.4 us -> 30.2 us
    unnamed x20 -> x0, local copies, waits for them, and re-layouts: 5.69 us -> none
    pallas_call x1 -> x2, Pallas kernels: 31.4 us -> 30.2 us  [the longest x1 28.7 us: local(): pl.pallas_call(functools.partial(kernel, sizes), out_shape=out_shape, in_...]
where the time goes in v2:
time: 31.1 us; the launch traced here: 30.8 us
  Pallas kernels  30.2 us (97%)
  between operations  0.64 us (2%)
    pallas_call x1, Pallas kernels, local(): pl.pallas_call(functools.partial(kernel, sizes), out_shape=out_shape, in_...  28.7 us
    pallas_call x1, Pallas kernels, local(): pl.pallas_call(write_out, out_shape=out_shape, in_specs=[vmem] * 3, out_s...  1.5 us

profile of v2, /device:TPU:1, one launch (start us, length us, event | category | flops | bytes accessed | tf_op | source)
XLA Modules:
  0.0 30.8 jit_solution(9116687258305011653)
XLA Ops:
  0.6 28.7 %bed_step.1 = (f32[3,16,128]{2,1,0:T(8,128)}, f32[3,16,128]{2,1,0:T(8,128)}, f32[3,4,8,128]{3,2,1,0:T(8,128)}) custom-call(f32[3,16,128]{2,1,0:T(8,128)} %pos_in.1, f32[3,16,128]{2,1,0:T(8,128)} %vel_in.1, f32[16,128]{1,0:T(8,128)} %wts_in.1, s32[16]{0:T(128)} %counts_in.1, s32[3,16]{1,0:T(4,128)} %bitcast.3, s32[3,16]{1,0:T(4,128)} %bitcast.4, ...), custom_call_target="tpu_custom_call" | custom-call | tf_op jit(solution)/shard_map/bed_step/pallas_call | solution.py:462
  29.4 1.5 %out_write.1 = (f32[3,16,128]{2,1,0:T(8,128)}, f32[3,16,128]{2,1,0:T(8,128)}, f32[3,4,8,128]{3,2,1,0:T(8,128)}) custom-call(f32[3,16,128]{2,1,0:T(8,128)} %get-tuple-element.6.refs_0_, f32[3,16,128]{2,1,0:T(8,128)} %get-tuple-element.7.refs_1_, f32[3,4,8,128]{3,2,1,0:T(8,128)} %get-tuple-element.8.refs_2_), custom_call_target="tpu_custom_call" | custom-call | tf_op jit(solution)/shard_map/out_write/pallas_call | solution.py:509

commit v3 on v2

--- a/solution.py
+++ b/solution.py
@@ -58,6 +58,7 @@
     aug,
     vals,
     sums,
+    pairs,
     req,
     answer,
     ans,
@@ -104,6 +105,17 @@
         (gx, gy, lax.rem(gz + ngz - 1, ngz)),
     )
 
+    barrier = pltpu.get_barrier_semaphore()
+
+    @pl.loop(1, group)
+    def _(k):
+        pl.semaphore_signal(
+            barrier, inc=1, device_id=in_group(lax.rem(me + k, group)), device_id_type=MESH
+        )
+
+    for other in (bin_right, bin_left, faces[4], faces[5]):
+        pl.semaphore_signal(barrier, inc=1, device_id=other, device_id_type=MESH)
+
     loads = [
         pltpu.make_async_copy(src, dst, load_sem.at[n])
         for n, (src, dst) in enumerate(
@@ -122,17 +134,6 @@
     ]
     for copy in loads:
         copy.start()
-
-    barrier = pltpu.get_barrier_semaphore()
-
-    @pl.loop(1, group)
-    def _(k):
-        pl.semaphore_signal(
-            barrier, inc=1, device_id=in_group(lax.rem(me + k, group)), device_id_type=MESH
-        )
-
-    for other in (bin_right, bin_left, faces[4], faces[5]):
-        pl.semaphore_signal(barrier, inc=1, device_id=other, device_id_type=MESH)
 
     row8, lane8 = iota((8, 128), 0), iota((8, 128), 1)
     row16, lane16 = iota((16, 128), 0), iota((16, 128), 1)
@@ -275,7 +276,7 @@
             ).astype(bf16)
 
     def prepare_own(wide):
-        @pl.loop(BINS, 2 * BINS)
+        @pl.loop(BINS, 2 * BINS, unroll=8)
         def _(slot):
             prepare(wide, slot, 1.0, True)
 
@@ -283,30 +284,41 @@
     has_right = jnp.where(here < devices - 1, 1.0, 0.0).astype(f32)
 
     def prepare_halo(wide):
-        @pl.loop(0, BINS)
+        @pl.loop(0, BINS, unroll=4)
         def _(slot):
             prepare(wide, slot, has_left, False)
             prepare(wide, slot + 2 * BINS, has_right, False)
 
-    def contact(b):
+    def near_of(b):
         slots = [b + BINS]
         for q in range(3):
             slots.append(jnp.where(lmask[q, b] != 0, b + BINS + loff[q, b], 3 * BINS))
-        near = jnp.concatenate([aug[s] for s in slots], axis=1)
-        value = jnp.concatenate([vals[s] for s in slots], axis=1)
-        exponent = lax.dot_general(
-            near, own_aug[b], (((0,), (0,)), ((), ())), preferred_element_type=f32
-        )
-        pair = jnp.exp2(exponent)
-        high = pair.astype(bf16)
-        low = (pair - high.astype(f32)).astype(bf16)
-        total = jnp.dot(value, high, preferred_element_type=f32)
-        total = total + jnp.dot(value, low, preferred_element_type=f32)
-        return total[0:8] + total[8:16] + total[16:24]
-
-    def advanced(tile, total, seen):
+        return slots
+
+    def contact():
+        @pl.loop(0, BINS, unroll=16)
+        def _(b):
+            near = jnp.concatenate([aug[s] for s in near_of(b)], axis=1)
+            exponent = lax.dot_general(
+                near, own_aug[b], (((0,), (0,)), ((), ())), preferred_element_type=f32
+            )
+            pair = jnp.exp2(exponent)
+            high = pair.astype(bf16)
+            pairs[b, 0:512] = high
+            pairs[b, 512:1024] = (pair - high.astype(f32)).astype(bf16)
+
+        @pl.loop(0, BINS, unroll=16)
+        def _(b):
+            value = jnp.concatenate([vals[s] for s in near_of(b)], axis=1)
+            total = jnp.dot(value, pairs[b, 0:512], preferred_element_type=f32)
+            total = total + jnp.dot(value, pairs[b, 512:1024], preferred_element_type=f32)
+            sums[b] = total[0:8] + total[8:16] + total[16:24]
+
+    def pushed_by(tile, total):
         net = tile * total[6:7, :] - total
-        force = STIFF * pltpu.roll(net, 3, 0) - DAMP * net
+        return STIFF * pltpu.roll(net, 3, 0) - DAMP * net
+
+    def advanced(tile, force, seen):
         held = STEP * tile[7:8, :]
         new_v = tile + held * (force + (seen - tile))
         new_x = tile + held * pltpu.roll(new_v, 5, 0)
@@ -370,33 +382,39 @@
         copy.wait_recv()
     prepare_halo(wide1)
 
-    @pl.loop(0, BINS, unroll=8)
-    def _(b):
-        sums[b] = contact(b)
+    contact()
+
+    drawn = jnp.zeros((8, 128), f32)
+    for b in range(BINS):
+        tile = wide1[BINS + b]
+        force = pushed_by(tile, sums[b])
+        held = STEP * tile[7:8, :]
+        term = jnp.where(row8 == 6, 2.0 - held, held * (tile - force) - 2.0 * tile)
+        drawn = jnp.where(
+            lane8 == b, jnp.sum(tile[6:7, :] * term, axis=1, keepdims=True), drawn
+        )
+        sums[b] = force
+    dep[me] = pltpu.roll(drawn, first_lane, 1)
+    group_start(2, dep, lambda other: dep.at[me])
 
     group_all(1, ans).wait_recv()
     seen = ans[0]
     for s in range(1, group):
         seen = seen + ans[s]
     seen = pltpu.roll(seen, lax.rem(128 - first_lane, 128), 1)
-    drawn = jnp.zeros((8, 128), f32)
     for b in range(BINS):
         seen_b = jnp.broadcast_to(seen[:, b : b + 1], (8, 128))
-        tile = wide1[BINS + b]
-        new = advanced(tile, sums[b], seen_b)
-        wide2[BINS + b] = new
-        drag = (seen_b - tile) + (seen_b - new)
-        pulled = jnp.sum(tile[6:7, :] * drag, axis=1, keepdims=True)
-        drawn = jnp.where(lane8 == b, pulled, drawn)
-    dep[me] = pltpu.roll(drawn, first_lane, 1)
+        wide2[BINS + b] = advanced(wide1[BINS + b], sums[b], seen_b)
     halo2 = halo_copies(1, wide2)
     for copy in halo2:
         copy.start()
-    group_start(2, dep, lambda other: dep.at[me])
     prepare_own(wide2)
 
     group_all(2, dep).wait_recv()
-    pushed = -COUPLING * gathered(dep)
+    drawn_all = gathered(dep)
+    there = [answer[t] for t in range(tiles)]
+    there = jnp.concatenate(there, axis=1) if tiles > 1 else there[0]
+    pushed = -COUPLING * (drawn_all[6:7, :] * there + drawn_all)
     spread = jnp.concatenate(
         [pushed[3 + c : 4 + c, :] * row_hot[...] for c in range(3)], axis=0
     )
@@ -414,14 +432,11 @@
         copy.wait_recv()
     prepare_halo(wide2)
 
-    @pl.loop(0, BINS, unroll=8)
-    def _(b):
-        sums[b] = contact(b)
+    contact()
 
     for b in range(BINS):
-        sums[b] = advanced(
-            wide2[BINS + b], sums[b], jnp.broadcast_to(seen[:, b : b + 1], (8, 128))
-        )
+        tile, seen_b = wide2[BINS + b], jnp.broadcast_to(seen[:, b : b + 1], (8, 128))
+        sums[b] = advanced(tile, pushed_by(tile, sums[b]), seen_b)
     for c in range(3):
         pos_out[c] = sums[:, c, :]
         vel_out[c] = sums[:, 3 + c, :]
@@ -480,6 +495,7 @@
                 pltpu.VMEM((3 * BINS + 1, 48, 128), bf16),
                 pltpu.VMEM((3 * BINS + 1, 32, 128), bf16),
                 pltpu.VMEM((BINS, 8, 128), f32),
+                pltpu.VMEM((BINS, 1024, 128), bf16),
                 pltpu.VMEM((group, 8, 128), i32),
                 pltpu.VMEM((tiles, 8, 128), f32),
                 pltpu.VMEM((group, 8, 128), f32),

time: 31.1 us -> 29.9 us (0.961)
  Pallas kernels: 30.2 us -> 29 us
    pallas_call x1, Pallas kernels: 28.7 us -> 27.5 us  [local(): pl.pallas_call(functools.partial(kernel, sizes), out_shape=out_shape, in_...]
where the time goes in v3:
time: 29.9 us; the launch traced here: 29.7 us
  Pallas kernels  29 us (97%)
  between operations  0.64 us (2%)
    pallas_call x1, Pallas kernels, local(): pl.pallas_call(functools.partial(kernel, sizes), out_shape=out_shape, in_...  27.5 us
    pallas_call x1, Pallas kernels, local(): pl.pallas_call(write_out, out_shape=out_shape, in_specs=[vmem] * 3, out_s...  1.5 us

profile of v3, /device:TPU:1, one launch (start us, length us, event | category | flops | bytes accessed | tf_op | source)
XLA Modules:
  0.0 29.7 jit_solution(185900213237367390)
XLA Ops:
  0.6 27.5 %bed_step.1 = (f32[3,16,128]{2,1,0:T(8,128)}, f32[3,16,128]{2,1,0:T(8,128)}, f32[3,4,8,128]{3,2,1,0:T(8,128)}) custom-call(f32[3,16,128]{2,1,0:T(8,128)} %pos_in.1, f32[3,16,128]{2,1,0:T(8,128)} %vel_in.1, f32[16,128]{1,0:T(8,128)} %wts_in.1, s32[16]{0:T(128)} %counts_in.1, s32[3,16]{1,0:T(4,128)} %bitcast.3, s32[3,16]{1,0:T(4,128)} %bitcast.4, ...), custom_call_target="tpu_custom_call" | custom-call | tf_op jit(solution)/shard_map/bed_step/pallas_call | solution.py:477
  28.2 1.5 %out_write.1 = (f32[3,16,128]{2,1,0:T(8,128)}, f32[3,16,128]{2,1,0:T(8,128)}, f32[3,4,8,128]{3,2,1,0:T(8,128)}) custom-call(f32[3,16,128]{2,1,0:T(8,128)} %get-tuple-element.6.refs_0_, f32[3,16,128]{2,1,0:T(8,128)} %get-tuple-element.7.refs_1_, f32[3,4,8,128]{3,2,1,0:T(8,128)} %get-tuple-element.8.refs_2_), custom_call_target="tpu_custom_call" | custom-call | tf_op jit(solution)/shard_map/out_write/pallas_call | solution.py:525

commit v4 on v3

--- a/solution.py
+++ b/solution.py
@@ -107,14 +107,14 @@
 
     barrier = pltpu.get_barrier_semaphore()
 
+    for other in (bin_right, bin_left, faces[4], faces[5]):
+        pl.semaphore_signal(barrier, inc=1, device_id=other, device_id_type=MESH)
+
     @pl.loop(1, group)
     def _(k):
         pl.semaphore_signal(
             barrier, inc=1, device_id=in_group(lax.rem(me + k, group)), device_id_type=MESH
         )
-
-    for other in (bin_right, bin_left, faces[4], faces[5]):
-        pl.semaphore_signal(barrier, inc=1, device_id=other, device_id_type=MESH)
 
     loads = [
         pltpu.make_async_copy(src, dst, load_sem.at[n])
@@ -243,10 +243,10 @@
 
     pl.semaphore_wait(barrier, group - 1 + 4)
 
-    group_start(0, req, lambda other: req.at[me])
     halo1 = halo_copies(0, wide1)
     for copy in halo1:
         copy.start()
+    group_start(0, req, lambda other: req.at[me])
     faces0 = face_copies(0, fluid)
     for copy in faces0:
         copy.start()
@@ -295,17 +295,26 @@
             slots.append(jnp.where(lmask[q, b] != 0, b + BINS + loff[q, b], 3 * BINS))
         return slots
 
+    def pair_kernel(b, slots, first):
+        near = jnp.concatenate([aug[s] for s in slots], axis=1)
+        exponent = lax.dot_general(
+            near, own_aug[b], (((0,), (0,)), ((), ())), preferred_element_type=f32
+        )
+        pair = jnp.exp2(exponent)
+        high = pair.astype(bf16)
+        size = 128 * len(slots)
+        pairs[b, first : first + size] = high
+        pairs[b, 512 + first : 512 + first + size] = (pair - high.astype(f32)).astype(bf16)
+
+    def contact_own():
+        @pl.loop(0, BINS, unroll=16)
+        def _(b):
+            pair_kernel(b, [b + BINS], 0)
+
     def contact():
         @pl.loop(0, BINS, unroll=16)
         def _(b):
-            near = jnp.concatenate([aug[s] for s in near_of(b)], axis=1)
-            exponent = lax.dot_general(
-                near, own_aug[b], (((0,), (0,)), ((), ())), preferred_element_type=f32
-            )
-            pair = jnp.exp2(exponent)
-            high = pair.astype(bf16)
-            pairs[b, 0:512] = high
-            pairs[b, 512:1024] = (pair - high.astype(f32)).astype(bf16)
+            pair_kernel(b, near_of(b)[1:], 128)
 
         @pl.loop(0, BINS, unroll=16)
         def _(b):
@@ -327,6 +336,7 @@
     aug[3 * BINS] = jnp.zeros((48, 128), bf16)
     vals[3 * BINS] = jnp.zeros((32, 128), bf16)
     prepare_own(wide1)
+    contact_own()
 
     group_all(0, req).wait_recv()
     asked_all = gathered(req)
@@ -372,12 +382,6 @@
         total = total + jnp.where(lane8 == 0, zl[:, k : k + 1], pltpu.roll(tile, 1, 1))
         return total + jnp.where(lane8 == 127, zr[:, k : k + 1], pltpu.roll(tile, 127, 1))
 
-    for copy in faces0:
-        copy.wait_recv()
-    for c in range(3):
-        for x in range(4):
-            rate_buf[c, x] = VISC * laplace(0, fluid, c, x)
-
     for copy in halo1:
         copy.wait_recv()
     prepare_halo(wide1)
@@ -396,6 +400,12 @@
         sums[b] = force
     dep[me] = pltpu.roll(drawn, first_lane, 1)
     group_start(2, dep, lambda other: dep.at[me])
+
+    for copy in faces0:
+        copy.wait_recv()
+    for c in range(3):
+        for x in range(4):
+            rate_buf[c, x] = VISC * laplace(0, fluid, c, x)
 
     group_all(1, ans).wait_recv()
     seen = ans[0]
@@ -409,6 +419,7 @@
     for copy in halo2:
         copy.start()
     prepare_own(wide2)
+    contact_own()
 
     group_all(2, dep).wait_recv()
     drawn_all = gathered(dep)
@@ -469,6 +480,7 @@
     tiles = -(-group * BINS // 128)
     vmem, anywhere = pl.BlockSpec(memory_space=pltpu.VMEM), pl.BlockSpec(memory_space=pltpu.HBM)
     dma = pltpu.SemaphoreType.DMA
+    args = (pos, vel, wts, counts, loff.T, lmask.T, bbox.T, bcell, fluid)
     out_shape = (
         jax.ShapeDtypeStruct((3, BINS, 128), f32),
         jax.ShapeDtypeStruct((3, BINS, 128), f32),
@@ -518,16 +530,17 @@
                 dma((2, 6)),
             ],
             compiler_params=pltpu.CompilerParams(
-                collective_id=0, has_side_effects=True, vmem_limit_bytes=60 * 2**20
+                collective_id=0, has_side_effects=True, vmem_limit_bytes=16 * 2**20
             ),
             name="bed_step",
-        )(pos, vel, wts, counts, loff.T, lmask.T, bbox.T, bcell, fluid)
+        )(*(pltpu.with_memory_space_constraint(x, pltpu.HBM) for x in args))
     return tuple(pl.pallas_call(
         write_out,
         out_shape=out_shape,
         in_specs=[vmem] * 3,
         out_specs=(anywhere,) * 3,
         scratch_shapes=[dma((3,))],
+        compiler_params=pltpu.CompilerParams(vmem_limit_bytes=4 * 2**20),
         name="out_write",
     )(*results))
 

time: 29.9 us -> 27.5 us (0.920)
  Pallas kernels: 29 us -> 26.7 us
    pallas_call x1, Pallas kernels: 27.5 us -> 26 us  [local(): pl.pallas_call(functools.partial(kernel, sizes), out_shape=out_shape, in_...]
    pallas_call x1, Pallas kernels: 1.5 us -> 0.67 us  [local(): pl.pallas_call(write_out, out_shape=out_shape, in_specs=[vmem] * 3, out_s...]
where the time goes in v4:
time: 27.5 us; the launch traced here: 27.3 us
  Pallas kernels  26.7 us (97%)
  between operations  0.64 us (2%)
    pallas_call x1, Pallas kernels, local(): pl.pallas_call(functools.partial(kernel, sizes), out_shape=out_shape, in_...  26 us
    pallas_call x1, Pallas kernels, local(): pl.pallas_call(write_out, out_shape=out_shape, in_specs=[vmem] * 3, out_s...  0.67 us

profile of v4, /device:TPU:1, one launch (start us, length us, event | category | flops | bytes accessed | tf_op | source)
XLA Modules:
  0.0 27.3 jit_solution(8806758763673272155)
XLA Ops:
  0.6 26.0 %bed_step.1 = (f32[3,16,128]{2,1,0:T(8,128)S(1)}, f32[3,16,128]{2,1,0:T(8,128)S(1)}, f32[3,4,8,128]{3,2,1,0:T(8,128)S(1)}) custom-call(f32[3,16,128]{2,1,0:T(8,128)} %pos_in.1, f32[3,16,128]{2,1,0:T(8,128)} %vel_in.1, f32[16,128]{1,0:T(8,128)} %wts_in.1, s32[16]{0:T(128)} %counts_in.1, s32[3,16]{1,0:T(4,128)} %bitcast.3, s32[3,16]{1,0:T(4,128)} %bitcast.4, ...), custom_call_target="tpu_custom_call" | custom-call | tf_op jit(solution)/shard_map/bed_step/pallas_call | solution.py:489
  26.7 0.7 %out_write.1 = (f32[3,16,128]{2,1,0:T(8,128)}, f32[3,16,128]{2,1,0:T(8,128)}, f32[3,4,8,128]{3,2,1,0:T(8,128)}) custom-call(f32[3,16,128]{2,1,0:T(8,128)S(1)} %get-tuple-element.6.refs_0_, f32[3,16,128]{2,1,0:T(8,128)S(1)} %get-tuple-element.7.refs_1_, f32[3,4,8,128]{3,2,1,0:T(8,128)S(1)} %get-tuple-element.8.refs_2_), custom_call_target="tpu_custom_call" | custom-call | tf_op jit(solution)/shard_map/out_write/pallas_call | solution.py:537

commit v5 on v4

--- a/solution.py
+++ b/solution.py
@@ -65,6 +65,7 @@
     dep,
     lane_hot,
     row_hot,
+    fluid_parts,
     rate_buf,
     first_buf,
     hx,
@@ -150,16 +151,19 @@
         )
     req[me] = asked
 
-    def face_sources(turn, field):
-        for side, (edge_row, edge_lane) in enumerate(((7, 127), (0, 0))):
-            rows, lanes = jnp.zeros((16, 128), f32), jnp.zeros((8, 128), f32)
-            for c in range(3):
-                for x in range(4):
-                    k = c * 4 + x
-                    tile = field[c, x]
-                    rows = jnp.where(row16 == k, tile[edge_row : edge_row + 1, :], rows)
-                    lanes = jnp.where(lane8 == k, tile[:, edge_lane : edge_lane + 1], lanes)
+    def pack_y(turn, field):
+        for side, edge in enumerate((7, 0)):
+            rows = jnp.zeros((16, 128), f32)
+            for k in range(12):
+                rows = jnp.where(row16 == k, field[k // 4, k % 4, edge : edge + 1, :], rows)
             sy[turn, side] = rows
+
+    def pack_z(turn, field):
+        for side, edge in enumerate((127, 0)):
+            lanes = jnp.zeros((8, 128), f32)
+            for k in range(12):
+                tile = field[k // 4, k % 4]
+                lanes = jnp.where(lane8 == k, tile[:, edge : edge + 1], lanes)
             sz[turn, side] = lanes
 
     def face_copies(turn, field):
@@ -184,11 +188,12 @@
         ]
 
     def halo_copies(turn, wide):
-        own = wide.at[pl.ds(BINS, BINS)]
+        rows = pl.ds(0, 6 if turn else 7)
+        own = wide.at[pl.ds(BINS, BINS), rows]
         return [
             pltpu.make_async_remote_copy(
                 src_ref=own,
-                dst_ref=wide.at[pl.ds(start, BINS)],
+                dst_ref=wide.at[pl.ds(start, BINS), rows],
                 send_sem=halo_send.at[turn, n],
                 recv_sem=halo_recv.at[turn, n],
                 device_id=other,
@@ -227,7 +232,9 @@
         return jnp.concatenate(out, axis=1) if tiles > 1 else out[0]
 
     loads[2].wait()
-    face_sources(0, fluid)
+    pack_y(0, fluid)
+    pack_z(0, fluid)
+    fluid_parts[...] = stacked(fluid[...].reshape(96, 128))
 
     for copy in loads[3:]:
         copy.wait()
@@ -253,7 +260,7 @@
 
     def prepare(wide, slot, scale, own):
         tile = wide[slot]
-        carried = tile[6:7, :] * scale
+        carried = wide1[slot, 6:7, :] * scale
         v = jnp.where(row8 < 6, tile, jnp.where(row8 == 6, 1.0, 0.0)) * carried
         vh, vm, vl = parts(v)
         vals[slot] = jnp.concatenate([vh, vm, vl, jnp.zeros_like(vh)], axis=0).astype(bf16)
@@ -283,11 +290,13 @@
     has_left = jnp.where(here > 0, 1.0, 0.0).astype(f32)
     has_right = jnp.where(here < devices - 1, 1.0, 0.0).astype(f32)
 
-    def prepare_halo(wide):
-        @pl.loop(0, BINS, unroll=4)
-        def _(slot):
-            prepare(wide, slot, has_left, False)
-            prepare(wide, slot + 2 * BINS, has_right, False)
+    def prepare_halo(wide, copies):
+        for copy, first, scale in zip(copies, (0, 2 * BINS), (has_left, has_right)):
+            copy.wait_recv()
+
+            @pl.loop(first, first + BINS, unroll=8)
+            def _(slot, scale=scale):
+                prepare(wide, slot, scale, False)
 
     def near_of(b):
         slots = [b + BINS]
@@ -311,17 +320,18 @@
         def _(b):
             pair_kernel(b, [b + BINS], 0)
 
+    def weigh(b):
+        value = jnp.concatenate([vals[s] for s in near_of(b)], axis=1)
+        total = jnp.dot(value, pairs[b, 0:512], preferred_element_type=f32)
+        total = total + jnp.dot(value, pairs[b, 512:1024], preferred_element_type=f32)
+        sums[b] = total[0:8] + total[8:16] + total[16:24]
+
     def contact():
-        @pl.loop(0, BINS, unroll=16)
-        def _(b):
-            pair_kernel(b, near_of(b)[1:], 128)
-
-        @pl.loop(0, BINS, unroll=16)
-        def _(b):
-            value = jnp.concatenate([vals[s] for s in near_of(b)], axis=1)
-            total = jnp.dot(value, pairs[b, 0:512], preferred_element_type=f32)
-            total = total + jnp.dot(value, pairs[b, 512:1024], preferred_element_type=f32)
-            sums[b] = total[0:8] + total[8:16] + total[16:24]
+        for b in range(BINS + 8):
+            if b < BINS:
+                pair_kernel(b, near_of(b)[1:], 128)
+            if b >= 8:
+                weigh(b - 8)
 
     def pushed_by(tile, total):
         net = tile * total[6:7, :] - total
@@ -349,7 +359,7 @@
         (iota((32, wide_lanes), 0) == (cell >> 7)) & (asked_all[0:1, :] == me), 1.0, 0.0
     ).astype(f32)
     at_lane = jnp.dot(
-        stacked(fluid[...].reshape(96, 128)), lane_hot[...], preferred_element_type=f32
+        fluid_parts[...], lane_hot[...], preferred_element_type=f32
     )
     at_lane = at_lane[0:96] + at_lane[96:192] + at_lane[192:288]
     reply = jnp.zeros((8, wide_lanes), f32)
@@ -366,25 +376,33 @@
     in_y = [jnp.where(g, 1.0, 0.0).astype(f32) for g in (gy > 0, gy < ngy - 1)]
     in_z = [jnp.where(g, 1.0, 0.0).astype(f32) for g in (gz > 0, gz < ngz - 1)]
 
-    def laplace(turn, field, c, x):
+    def laplace_inside(field, c, x):
+        tile = field[c, x]
+        total = -6.0 * tile
+        if x > 0:
+            total = total + field[c, x - 1]
+        if x < 3:
+            total = total + field[c, x + 1]
+        total = total + jnp.where(row8 == 0, 0.0, pltpu.roll(tile, 1, 0))
+        total = total + jnp.where(row8 == 7, 0.0, pltpu.roll(tile, 7, 0))
+        total = total + jnp.where(lane8 == 0, 0.0, pltpu.roll(tile, 1, 1))
+        return total + jnp.where(lane8 == 127, 0.0, pltpu.roll(tile, 127, 1))
+
+    def laplace_edges(turn, c, x):
         k = c * 4 + x
-        tile = field[c, x]
-        below = field[c, x - 1] if x > 0 else hx[turn, 0, c] * in_x[0]
-        above = field[c, x + 1] if x < 3 else hx[turn, 1, c] * in_x[1]
-        total = below + above - 6.0 * tile
+        y0, y7 = hy[turn, 0, k : k + 1, :] * in_y[0], hy[turn, 1, k : k + 1, :] * in_y[1]
+        z0, z127 = hz[turn, 0] * in_z[0], hz[turn, 1] * in_z[1]
+        total = jnp.where(row8 == 0, y0, jnp.where(row8 == 7, y7, 0.0))
         total = total + jnp.where(
-            row8 == 0, hy[turn, 0, k : k + 1, :] * in_y[0], pltpu.roll(tile, 1, 0)
-        )
-        total = total + jnp.where(
-            row8 == 7, hy[turn, 1, k : k + 1, :] * in_y[1], pltpu.roll(tile, 7, 0)
-        )
-        zl, zr = hz[turn, 0] * in_z[0], hz[turn, 1] * in_z[1]
-        total = total + jnp.where(lane8 == 0, zl[:, k : k + 1], pltpu.roll(tile, 1, 1))
-        return total + jnp.where(lane8 == 127, zr[:, k : k + 1], pltpu.roll(tile, 127, 1))
-
-    for copy in halo1:
-        copy.wait_recv()
-    prepare_halo(wide1)
+            lane8 == 0, z0[:, k : k + 1], jnp.where(lane8 == 127, z127[:, k : k + 1], 0.0)
+        )
+        if x == 0:
+            total = total + hx[turn, 0, c] * in_x[0]
+        if x == 3:
+            total = total + hx[turn, 1, c] * in_x[1]
+        return total
+
+    prepare_halo(wide1, halo1)
 
     contact()
 
@@ -405,7 +423,7 @@
         copy.wait_recv()
     for c in range(3):
         for x in range(4):
-            rate_buf[c, x] = VISC * laplace(0, fluid, c, x)
+            rate_buf[c, x] = VISC * (laplace_inside(fluid, c, x) + laplace_edges(0, c, x))
 
     group_all(1, ans).wait_recv()
     seen = ans[0]
@@ -434,14 +452,20 @@
     )
     source = source[0:96] + source[96:192] + source[192:288]
     first_buf[...] = rate_buf[...] + source.reshape(3, 4, 8, 128)
-    face_sources(1, first_buf)
     faces1 = face_copies(1, first_buf)
-    for copy in faces1:
-        copy.start()
-
-    for copy in halo2:
-        copy.wait_recv()
-    prepare_halo(wide2)
+    pack_z(1, first_buf)
+    for copy in (*faces1[4:], *faces1[:2]):
+        copy.start()
+    pack_y(1, first_buf)
+    for copy in faces1[2:4]:
+        copy.start()
+    for c in range(3):
+        for x in range(4):
+            rate_buf[c, x] = (
+                fluid[c, x] + first_buf[c, x] + (0.5 * VISC) * laplace_inside(first_buf, c, x)
+            )
+
+    prepare_halo(wide2, halo2)
 
     contact()
 
@@ -456,9 +480,7 @@
         copy.wait_recv()
     for c in range(3):
         for x in range(4):
-            fluid_out[c, x] = (
-                fluid[c, x] + first_buf[c, x] + (0.5 * VISC) * laplace(1, first_buf, c, x)
-            )
+            fluid_out[c, x] = rate_buf[c, x] + (0.5 * VISC) * laplace_edges(1, c, x)
 
     for copy in (*halo1, *faces0, *halo2, *faces1):
         copy.wait_send()
@@ -514,6 +536,7 @@
                 pltpu.VMEM((group, 8, 128), f32),
                 pltpu.VMEM((128, 128 * tiles), bf16),
                 pltpu.VMEM((32, 128 * tiles), f32),
+                pltpu.VMEM((288, 128), bf16),
                 pltpu.VMEM((3, 4, 8, 128), f32),
                 pltpu.VMEM((3, 4, 8, 128), f32),
                 pltpu.VMEM((2, 2, 3, 8, 128), f32),

time: 27.5 us -> 27.1 us (0.985)
  Pallas kernels: 26.7 us -> 26.3 us
    pallas_call x1, Pallas kernels: 26 us -> 25.6 us  [local(): pl.pallas_call(functools.partial(kernel, sizes), out_shape=out_shape, in_...]
where the time goes in v5:
time: 27.1 us; the launch traced here: 26.9 us
  Pallas kernels  26.3 us (97%)
  between operations  0.64 us (2%)
    pallas_call x1, Pallas kernels, local(): pl.pallas_call(functools.partial(kernel, sizes), out_shape=out_shape, in_...  25.6 us
    pallas_call x1, Pallas kernels, local(): pl.pallas_call(write_out, out_shape=out_shape, in_specs=[vmem] * 3, out_s...  0.67 us

profile of v5, /device:TPU:1, one launch (start us, length us, event | category | flops | bytes accessed | tf_op | source)
XLA Modules:
  0.0 26.9 jit_solution(10867669539513846360)
XLA Ops:
  0.6 25.6 %bed_step.1 = (f32[3,16,128]{2,1,0:T(8,128)S(1)}, f32[3,16,128]{2,1,0:T(8,128)S(1)}, f32[3,4,8,128]{3,2,1,0:T(8,128)S(1)}) custom-call(f32[3,16,128]{2,1,0:T(8,128)} %pos_in.1, f32[3,16,128]{2,1,0:T(8,128)} %vel_in.1, f32[16,128]{1,0:T(8,128)} %wts_in.1, s32[16]{0:T(128)} %counts_in.1, s32[3,16]{1,0:T(4,128)} %bitcast.3, s32[3,16]{1,0:T(4,128)} %bitcast.4, ...), custom_call_target="tpu_custom_call" | custom-call | tf_op jit(solution)/shard_map/bed_step/pallas_call | solution.py:511
  26.2 0.7 %out_write.1 = (f32[3,16,128]{2,1,0:T(8,128)}, f32[3,16,128]{2,1,0:T(8,128)}, f32[3,4,8,128]{3,2,1,0:T(8,128)}) custom-call(f32[3,16,128]{2,1,0:T(8,128)S(1)} %get-tuple-element.6.refs_0_, f32[3,16,128]{2,1,0:T(8,128)S(1)} %get-tuple-element.7.refs_1_, f32[3,4,8,128]{3,2,1,0:T(8,128)S(1)} %get-tuple-element.8.refs_2_), custom_call_target="tpu_custom_call" | custom-call | tf_op jit(solution)/shard_map/out_write/pallas_call | solution.py:560

commit v6 on v5

--- a/solution.py
+++ b/solution.py
@@ -187,18 +187,20 @@
             for n, (src, dst) in enumerate(pairs)
         ]
 
+    half = BINS // 2
+
     def halo_copies(turn, wide):
         rows = pl.ds(0, 6 if turn else 7)
-        own = wide.at[pl.ds(BINS, BINS), rows]
         return [
             pltpu.make_async_remote_copy(
-                src_ref=own,
-                dst_ref=wide.at[pl.ds(start, BINS), rows],
-                send_sem=halo_send.at[turn, n],
-                recv_sem=halo_recv.at[turn, n],
+                src_ref=wide.at[pl.ds(BINS + part * half, half), rows],
+                dst_ref=wide.at[pl.ds(start + part * half, half), rows],
+                send_sem=halo_send.at[turn, 2 * part + n],
+                recv_sem=halo_recv.at[turn, 2 * part + n],
                 device_id=other,
                 device_id_type=MESH,
             )
+            for part in range(2)
             for n, (start, other) in enumerate(((0, bin_right), (2 * BINS, bin_left)))
         ]
 
@@ -212,14 +214,20 @@
             device_id_type=MESH,
         )
 
+    group_rows = (pl.ds(0, 2), pl.ds(3, 3), pl.ds(3, 4))
+
     def group_start(turn, buffer, source):
+        rows = group_rows[turn]
+
         @pl.loop(1, group)
         def _(k):
             other = lax.rem(me + k, group)
-            group_copy(turn, source(other), buffer.at[me], in_group(other)).start()
+            group_copy(
+                turn, source(other).at[rows], buffer.at[me, rows], in_group(other)
+            ).start()
 
     def group_all(turn, buffer):
-        most = buffer.at[pl.ds(0, group - 1)]
+        most = buffer.at[pl.ds(0, group - 1), group_rows[turn]]
         return group_copy(turn, most, most, in_group(lax.rem(me + 1, group)))
 
     def gathered(buffer):
@@ -291,12 +299,13 @@
     has_right = jnp.where(here < devices - 1, 1.0, 0.0).astype(f32)
 
     def prepare_halo(wide, copies):
-        for copy, first, scale in zip(copies, (0, 2 * BINS), (has_left, has_right)):
+        for n, copy in enumerate(copies):
+            first, scale = ((0, has_left), (2 * BINS, has_right))[n % 2]
             copy.wait_recv()
 
-            @pl.loop(first, first + BINS, unroll=8)
-            def _(slot, scale=scale):
-                prepare(wide, slot, scale, False)
+            @pl.loop(0, half, unroll=half)
+            def _(b, first=first + (n // 2) * half, scale=scale):
+                prepare(wide, first + b, scale, False)
 
     def near_of(b):
         slots = [b + BINS]
@@ -545,8 +554,8 @@
                 pltpu.VMEM((2, 2, 16, 128), f32),
                 pltpu.VMEM((2, 2, 8, 128), f32),
                 dma((9,)),
-                dma((2, 2)),
-                dma((2, 2)),
+                dma((2, 4)),
+                dma((2, 4)),
                 dma((3,)),
                 dma((3,)),
                 dma((2, 6)),

time: 27.1 us -> 26.9 us (level)
  Pallas kernels: 26.3 us -> 26 us
where the time goes in v6:
time: 26.9 us; the launch traced here: 26.7 us
  Pallas kernels  26 us (97%)
  between operations  0.64 us (2%)
    pallas_call x1, Pallas kernels, local(): pl.pallas_call(functools.partial(kernel, sizes), out_shape=out_shape, in_...  25.4 us
    pallas_call x1, Pallas kernels, local(): pl.pallas_call(write_out, out_shape=out_shape, in_specs=[vmem] * 3, out_s...  0.67 us

profile of v6, /device:TPU:1, one launch (start us, length us, event | category | flops | bytes accessed | tf_op | source)
XLA Modules:
  0.0 26.7 jit_solution(14419031833081081434)
XLA Ops:
  0.6 25.4 %bed_step.1 = (f32[3,16,128]{2,1,0:T(8,128)S(1)}, f32[3,16,128]{2,1,0:T(8,128)S(1)}, f32[3,4,8,128]{3,2,1,0:T(8,128)S(1)}) custom-call(f32[3,16,128]{2,1,0:T(8,128)} %pos_in.1, f32[3,16,128]{2,1,0:T(8,128)} %vel_in.1, f32[16,128]{1,0:T(8,128)} %wts_in.1, s32[16]{0:T(128)} %counts_in.1, s32[3,16]{1,0:T(4,128)} %bitcast.3, s32[3,16]{1,0:T(4,128)} %bitcast.4, ...), custom_call_target="tpu_custom_call" | custom-call | tf_op jit(solution)/shard_map/bed_step/pallas_call | solution.py:520
  26.0 0.7 %out_write.1 = (f32[3,16,128]{2,1,0:T(8,128)}, f32[3,16,128]{2,1,0:T(8,128)}, f32[3,4,8,128]{3,2,1,0:T(8,128)}) custom-call(f32[3,16,128]{2,1,0:T(8,128)S(1)} %get-tuple-element.6.refs_0_, f32[3,16,128]{2,1,0:T(8,128)S(1)} %get-tuple-element.7.refs_1_, f32[3,4,8,128]{3,2,1,0:T(8,128)S(1)} %get-tuple-element.8.refs_2_), custom_call_target="tpu_custom_call" | custom-call | tf_op jit(solution)/shard_map/out_write/pallas_call | solution.py:569

commit v7 on v6

--- a/solution.py
+++ b/solution.py
@@ -219,8 +219,7 @@
     def group_start(turn, buffer, source):
         rows = group_rows[turn]
 
-        @pl.loop(1, group)
-        def _(k):
+        for k in sorted(range(1, group), key=lambda k: -min(k % ngy, -k % ngy)):
             other = lax.rem(me + k, group)
             group_copy(
                 turn, source(other).at[rows], buffer.at[me, rows], in_group(other)

time: 26.9 us -> 26.9 us (level)
  no operation moved by 1% of the time
where the time goes in v7:
time: 26.9 us; the launch traced here: 26.7 us
  Pallas kernels  26.1 us (97%)
  between operations  0.64 us (2%)
    pallas_call x1, Pallas kernels, local(): pl.pallas_call(functools.partial(kernel, sizes), out_shape=out_shape, in_...  25.4 us
    pallas_call x1, Pallas kernels, local(): pl.pallas_call(write_out, out_shape=out_shape, in_specs=[vmem] * 3, out_s...  0.67 us

profile of v7, /device:TPU:1, one launch (start us, length us, event | category | flops | bytes accessed | tf_op | source)
XLA Modules:
  0.0 26.7 jit_solution(7466846477753831309)
XLA Ops:
  0.6 25.4 %bed_step.1 = (f32[3,16,128]{2,1,0:T(8,128)S(1)}, f32[3,16,128]{2,1,0:T(8,128)S(1)}, f32[3,4,8,128]{3,2,1,0:T(8,128)S(1)}) custom-call(f32[3,16,128]{2,1,0:T(8,128)} %pos_in.1, f32[3,16,128]{2,1,0:T(8,128)} %vel_in.1, f32[16,128]{1,0:T(8,128)} %wts_in.1, s32[16]{0:T(128)} %counts_in.1, s32[3,16]{1,0:T(4,128)} %bitcast.3, s32[3,16]{1,0:T(4,128)} %bitcast.4, ...), custom_call_target="tpu_custom_call" | custom-call | tf_op jit(solution)/shard_map/bed_step/pallas_call | solution.py:519
  26.1 0.7 %out_write.1 = (f32[3,16,128]{2,1,0:T(8,128)}, f32[3,16,128]{2,1,0:T(8,128)}, f32[3,4,8,128]{3,2,1,0:T(8,128)}) custom-call(f32[3,16,128]{2,1,0:T(8,128)S(1)} %get-tuple-element.6.refs_0_, f32[3,16,128]{2,1,0:T(8,128)S(1)} %get-tuple-element.7.refs_1_, f32[3,4,8,128]{3,2,1,0:T(8,128)S(1)} %get-tuple-element.8.refs_2_), custom_call_target="tpu_custom_call" | custom-call | tf_op jit(solution)/shard_map/out_write/pallas_call | solution.py:568
